TPU v7x, 32 devices: a whole 2x2x4 slice. The times are simulated.
32 devices in a mesh: ctx: 8 (over z, x), grp: 4 (over y, core).
Axes of the slice: x: 2, y: 2, z: 4, core: 2. Of those that a mesh axis runs over, the one named last changes fastest.
Arguments:
- queries: bfloat16 [1024, 64, 128], P('ctx', 'grp'), parts along dimension 1, may hold values from -4.6 to 4.6
- keys: bfloat16 [1024, 512], P('ctx', 'grp'), parts along dimension 1, may hold values from -4.6 to 4.6
- values: bfloat16 [1024, 512], P('ctx', 'grp'), parts along dimension 1, may hold values from -6 to 6
- grad_out: bfloat16 [1024, 64, 128], P('ctx', 'grp'), parts along dimension 1, may hold values from -6 to 6
- lengths: int32 [16], replicated, may hold values from 1 to 640, 1024 in all
Outputs:
- grad_queries: bfloat16 [1024, 64, 128], P('ctx', 'grp'), parts along dimension 1
- grad_keys: bfloat16 [1024, 512], P('ctx', 'grp'), parts along dimension 1
- grad_values: bfloat16 [1024, 512], P('ctx', 'grp'), parts along dimension 1
There are 4 independent parts, one for each index of `grp`. A program takes and returns all parts, laid end to end along the dimension named above; an argument that names none is the same for every part. Nothing has to cross between parts.
Inputs may be any that keep to these rules, and one draw needn't show every extreme that they name: `lengths`: the 16 documents lie end to end in the given order and fill the pack; the longest has exactly 640 tokens.
All inputs are finite; a program needn't handle non-finite values.
Results may differ from a plain program's by a relative error of at most 0.015.
Values may be sent and summed in bfloat16 or wider, within the bound.
No kernel may reach another device: no remote copies, remote signals or barrier semaphores. Data moves between devices by JAX's collectives and lax.ppermute only.
A program may use at most 64 MiB of HBM per device.

v0:
```python
import functools
import math

import jax
import jax.numpy as jnp
from jax import lax
from jax.experimental import pallas as pl
from jax.experimental.pallas import tpu as pltpu
from jax.sharding import PartitionSpec as P

NT = (((1,), (1,)), ((), ()))
TILE = 256


def attend(back, heads, lengths, start, *refs):
    q_ref, g_ref = refs[0], refs[1]
    kv_refs = refs[2 : 3 + back]
    dq_ref, own_ref = refs[3 + back], refs[4 + back]
    sent = refs[5 + back : 5 + 2 * back]
    acc = refs[5 + 2 * back]
    block = kv_refs[0].shape[0] // 2
    width = q_ref.shape[1]
    scale = 1.0 / math.sqrt(width)
    to_exp2 = scale * math.log2(math.e)
    first = start[0]

    def tile(index, carry):
        at = pl.ds(pl.multiple_of(index * TILE, TILE), TILE)
        q, g = q_ref[at, :], g_ref[at, :]
        row = lax.broadcasted_iota(jnp.int32, (1, TILE), 1) + index * TILE
        pos = first + lax.div(row, heads)
        low, end = jnp.zeros_like(pos), jnp.int32(0)
        for n in range(lengths.shape[0]):
            end = end + lengths[n]
            low = jnp.where(end <= pos, jnp.maximum(low, end), low)
        key = lax.broadcasted_iota(jnp.int32, (block, TILE), 0)
        scores, top = [], None
        for b in range(back + 1):
            s = lax.dot_general(kv_refs[b][:block, :], q, NT, preferred_element_type=jnp.float32)
            base = first - b * block
            allowed = (key >= low - base) & (key <= pos - base) if b == 0 else key >= low - base
            s = jnp.where(allowed, s, -1e30)
            high = jnp.max(s, axis=0, keepdims=True)
            top = high if top is None else jnp.maximum(top, high)
            scores.append(s)
        total, weighted, exps, grads = 0.0, 0.0, [], []
        for b in range(back + 1):
            e = jnp.exp2((scores[b] - top) * to_exp2)
            gp = lax.dot_general(kv_refs[b][block:, :], g, NT, preferred_element_type=jnp.float32)
            total = total + jnp.sum(e, axis=0, keepdims=True)
            weighted = weighted + jnp.sum(e * gp, axis=0, keepdims=True)
            exps.append(e)
            grads.append(gp)
        inverse = 1.0 / total
        delta = weighted * inverse
        dq = None
        for b in range(back + 1):
            p = exps[b] * inverse
            ds = (p * (grads[b] - delta)).astype(jnp.bfloat16)
            dk = jnp.dot(ds, q, preferred_element_type=jnp.float32)
            dv = jnp.dot(p.astype(jnp.bfloat16), g, preferred_element_type=jnp.float32)
            acc[b, :block, :] += dk
            acc[b, block:, :] += dv
            part = lax.dot_general(
                ds, kv_refs[b][:block, :], (((0,), (0,)), ((), ())), preferred_element_type=jnp.float32
            )
            dq = part if dq is None else dq + part
        dq_ref[at, :] = (dq * scale).astype(dq_ref.dtype)
        return carry

    acc[...] = jnp.zeros_like(acc)
    lax.fori_loop(0, q_ref.shape[0] // TILE, tile, 0)
    for b in range(back + 1):
        out = own_ref if b == 0 else sent[b - 1]
        out[:block, :] = (acc[b, :block, :] * scale).astype(out.dtype)
        out[block:, :] = acc[b, block:, :].astype(out.dtype)


def combine(*refs):
    own, rest, (dk, dv) = refs[0], refs[1:-2], refs[-2:]
    block = dk.shape[0]
    total = own[...]
    for r in rest:
        total = total + r[...].astype(jnp.float32)
    dk[...] = total[:block].astype(dk.dtype)
    dv[...] = total[block:].astype(dv.dtype)


def on_device(queries, keys, values, grad_out, lengths):
    rows, heads, width = queries.shape
    count = lax.axis_size("ctx")
    longest = rows * count // 2 + rows
    back = min(count - 1, -(-(longest - 1) // rows))
    start = (lax.axis_index("ctx") * rows).astype(jnp.int32).reshape(1)
    vmem, smem = pl.BlockSpec(memory_space=pltpu.VMEM), pl.BlockSpec(memory_space=pltpu.SMEM)

    def turn(x, by):
        return lax.ppermute(x, "ctx", [(i, (i + by) % count) for i in range(count)])

    pair = jnp.concatenate([keys, values], axis=0)
    blocks = [pair] + [turn(pair, b) for b in range(1, back + 1)]
    outs = pl.pallas_call(
        functools.partial(attend, back, heads),
        out_shape=[
            jax.ShapeDtypeStruct((rows * heads, width), jnp.bfloat16),
            jax.ShapeDtypeStruct((2 * rows, width), jnp.float32),
        ]
        + [jax.ShapeDtypeStruct((2 * rows, width), jnp.bfloat16)] * back,
        in_specs=[smem, smem] + [vmem] * (back + 3),
        out_specs=[vmem] * (back + 2),
        scratch_shapes=[pltpu.VMEM((back + 1, 2 * rows, width), jnp.float32)],
        compiler_params=pltpu.CompilerParams(vmem_limit_bytes=48 * 2**20),
    )(lengths, start, queries.reshape(-1, width), grad_out.reshape(-1, width), *blocks)
    returned = [turn(outs[1 + b], -b) for b in range(1, back + 1)]
    dk, dv = pl.pallas_call(
        combine,
        out_shape=[jax.ShapeDtypeStruct((rows, width), jnp.bfloat16)] * 2,
        in_specs=[vmem] * (back + 1),
        out_specs=[vmem] * 2,
    )(outs[1], *returned)
    return outs[0].reshape(queries.shape), dk, dv


def solution(mesh):
    return jax.shard_map(
        on_device,
        mesh=mesh,
        in_specs=(
            P("ctx", "grp", None),
            P("ctx", "grp"),
            P("ctx", "grp"),
            P("ctx", "grp", None),
            P(),
        ),
        out_specs=(P("ctx", "grp", None), P("ctx", "grp"), P("ctx", "grp")),
        check_vma=False,
    )
```

profile of v0, /device:TPU:0, one launch (start us, length us, event | category | flops | bytes accessed | tf_op | source)
XLA Modules:
  0.0 46.6 jit_solution(18131192425127592074)
XLA Ops:
  0.6 0.0 copy-start.9
  0.6 0.8 %constant_dynamic-update-slice_fusion.1 = bf16[256,128]{1,0:T(8,128)(2,1)S(1)} fusion(bf16[128,128]{1,0:T(8,128)(2,1)} %param.6), kind=kLoop, calls=%fused_computation.1 | loop fusion | bytes 65536
  1.4 0.0 copy-done.9
  1.4 5.0 %collective-permute-start.4 = (bf16[256,128]{1,0:T(8,128)(2,1)S(1)}, bf16[256,128]{1,0:T(8,128)(2,1)S(1)}, u32[]{:S(2)}, u32[]{:S(2)}) collective-permute-start(bf16[256,128]{1,0:T(8,128)(2,1)S(1)} %constant_dynamic-update-slice_fusion.refs_2_), channel_id=1, source_target_pairs={{0,20},{4,24},{8,28},{12,0},{16,4},{20,8},{24,12},{28,16},{1,21},{... | collective-permute-start | bytes 196616 | tf_op jit(solution)/shard_map/ppermute | solution.py:98
  6.4 0.3 collective-permute-start.3
  6.8 1.7 %collective-permute-start.2 = (bf16[256,128]{1,0:T(8,128)(2,1)S(1)}, bf16[256,128]{1,0:T(8,128)(2,1)S(1)}, u32[]{:S(2)}, u32[]{:S(2)}) collective-permute-start(bf16[256,128]{1,0:T(8,128)(2,1)S(1)} %constant_dynamic-update-slice_fusion.refs_2_), channel_id=1, source_target_pairs={{0,12},{4,16},{8,20},{12,24},{16,28},{20,0},{24,4},{28,8},{1,13},{... | collective-permute-start | bytes 196616 | tf_op jit(solution)/shard_map/ppermute | solution.py:98
  8.4 2.5 %collective-permute-start.1 = (bf16[256,128]{1,0:T(8,128)(2,1)S(1)}, bf16[256,128]{1,0:T(8,128)(2,1)S(1)}, u32[]{:S(2)}, u32[]{:S(2)}) collective-permute-start(bf16[256,128]{1,0:T(8,128)(2,1)S(1)} %constant_dynamic-update-slice_fusion.refs_2_), channel_id=1, source_target_pairs={{0,8},{4,12},{8,16},{12,20},{16,24},{20,28},{24,0},{28,4},{1,9},{5... | collective-permute-start | bytes 196616 | tf_op jit(solution)/shard_map/ppermute | solution.py:98
  10.9 1.5 %collective-permute-start = (bf16[256,128]{1,0:T(8,128)(2,1)S(1)}, bf16[256,128]{1,0:T(8,128)(2,1)S(1)}, u32[]{:S(2)}, u32[]{:S(2)}) collective-permute-start(bf16[256,128]{1,0:T(8,128)(2,1)S(1)} %constant_dynamic-update-slice_fusion.refs_2_), channel_id=1, source_target_pairs={{0,4},{4,8},{8,12},{12,16},{16,20},{20,24},{24,28},{28,0},{1,5},{5... | collective-permute-start | bytes 196616 | tf_op jit(solution)/shard_map/ppermute | solution.py:98
  12.4 0.0 collective-permute-done.4.refs_7_
  12.4 3.5 %collective-permute-done.3.refs_6_ = bf16[256,128]{1,0:T(8,128)(2,1)S(1)} collective-permute-done((bf16[256,128]{1,0:T(8,128)(2,1)S(1)}, bf16[256,128]{1,0:T(8,128)(2,1)S(1)}, u32[]{:S(2)}, u32[]{:S(2)}) %collective-permute-start.3) | collective-permute-done | bytes 65568 | tf_op jit(solution)/shard_map/ppermute | solution.py:98
  15.9 2.2 %collective-permute-done.2.refs_5_ = bf16[256,128]{1,0:T(8,128)(2,1)S(1)} collective-permute-done((bf16[256,128]{1,0:T(8,128)(2,1)S(1)}, bf16[256,128]{1,0:T(8,128)(2,1)S(1)}, u32[]{:S(2)}, u32[]{:S(2)}) %collective-permute-start.2) | collective-permute-done | bytes 65568 | tf_op jit(solution)/shard_map/ppermute | solution.py:98
  18.1 0.0 collective-permute-done.1.refs_4_
  18.1 0.0 collective-permute-done.refs_3_
  18.1 0.7 %copy-done.3 = s32[16]{0:T(128)S(1)} copy-done((s32[16]{0:T(128)S(1)}, s32[16]{0:T(128)}, u32[]{:S(2)}) %copy-start.3) | copy-done | bytes 88
  18.8 1.0 %copy-done = bf16[128,16,128]{2,1,0:T(8,128)(2,1)S(1)} copy-done((bf16[128,16,128]{2,1,0:T(8,128)(2,1)S(1)}, bf16[128,16,128]{2,1,0:T(8,128)(2,1)}, u32[]{:S(2)}) %copy-start) | copy-done | bytes 524312
  19.8 1.0 %copy-done.1 = bf16[128,16,128]{2,1,0:T(8,128)(2,1)S(1)} copy-done((bf16[128,16,128]{2,1,0:T(8,128)(2,1)S(1)}, bf16[128,16,128]{2,1,0:T(8,128)(2,1)}, u32[]{:S(2)}) %copy-start.1) | copy-done | bytes 524312
  20.9 10.1 %shard_map.76 = (bf16[2048,128]{1,0:T(8,128)(2,1)}, f32[256,128]{1,0:T(8,128)S(1)}, bf16[256,128]{1,0:T(8,128)(2,1)S(1)}, bf16[256,128]{1,0:T(8,128)(2,1)S(1)}, ...) custom-call(s32[16]{0:T(128)S(1)} %copy-done.3, s32[1]{0:T(128)} %bitcast.start, ...), custom_call_target="tpu_custom_call" | custom-call | tf_op jit(solution)/shard_map/pallas_call | solution.py:102
  31.0 0.6 %copy-done.2 = f32[256,128]{1,0:T(8,128)} copy-done((f32[256,128]{1,0:T(8,128)}, f32[256,128]{1,0:T(8,128)S(1)}, u32[]{:S(2)}) %copy-start.2) | copy-done | bytes 131096
  31.6 0.4 collective-permute-start.5
  32.0 2.1 %collective-permute-start.6 = (bf16[256,128]{1,0:T(8,128)(2,1)S(1)}, bf16[256,128]{1,0:T(8,128)(2,1)S(1)}, u32[]{:S(2)}, u32[]{:S(2)}) collective-permute-start(bf16[256,128]{1,0:T(8,128)(2,1)S(1)} %get-tuple-element.15), channel_id=1, source_target_pairs={{0,24},{4,28},{8,0},{12,4},{16,8},{20,12},{24,16},{28,20},{1,25},{... | collective-permute-start | bytes 196616 | tf_op jit(solution)/shard_map/ppermute | solution.py:98
  34.1 0.8 %collective-permute-start.7 = (bf16[256,128]{1,0:T(8,128)(2,1)S(1)}, bf16[256,128]{1,0:T(8,128)(2,1)S(1)}, u32[]{:S(2)}, u32[]{:S(2)}) collective-permute-start(bf16[256,128]{1,0:T(8,128)(2,1)S(1)} %get-tuple-element.16), channel_id=1, source_target_pairs={{0,20},{4,24},{8,28},{12,0},{16,4},{20,8},{24,12},{28,16},{1,21},{... | collective-permute-start | bytes 196616 | tf_op jit(solution)/shard_map/ppermute | solution.py:98
  34.9 1.8 %collective-permute-start.8 = (bf16[256,128]{1,0:T(8,128)(2,1)S(1)}, bf16[256,128]{1,0:T(8,128)(2,1)S(1)}, u32[]{:S(2)}, u32[]{:S(2)}) collective-permute-start(bf16[256,128]{1,0:T(8,128)(2,1)S(1)} %get-tuple-element.17), channel_id=1, source_target_pairs={{0,16},{4,20},{8,24},{12,28},{16,0},{20,4},{24,8},{28,12},{1,17},{... | collective-permute-start | bytes 196616 | tf_op jit(solution)/shard_map/ppermute | solution.py:98
  36.6 0.4 collective-permute-start.9
  37.0 0.0 collective-permute-done.5.refs_1_
  37.0 0.0 collective-permute-done.6.refs_2_
  37.0 2.4 %collective-permute-done.7.refs_3_ = bf16[256,128]{1,0:T(8,128)(2,1)S(1)} collective-permute-done((bf16[256,128]{1,0:T(8,128)(2,1)S(1)}, bf16[256,128]{1,0:T(8,128)(2,1)S(1)}, u32[]{:S(2)}, u32[]{:S(2)}) %collective-permute-start.7) | collective-permute-done | bytes 65568 | tf_op jit(solution)/shard_map/ppermute | solution.py:98
  39.5 4.1 %collective-permute-done.8.refs_4_ = bf16[256,128]{1,0:T(8,128)(2,1)S(1)} collective-permute-done((bf16[256,128]{1,0:T(8,128)(2,1)S(1)}, bf16[256,128]{1,0:T(8,128)(2,1)S(1)}, u32[]{:S(2)}, u32[]{:S(2)}) %collective-permute-start.8) | collective-permute-done | bytes 65568 | tf_op jit(solution)/shard_map/ppermute | solution.py:98
  43.6 0.6 %collective-permute-done.9.refs_5_ = bf16[256,128]{1,0:T(8,128)(2,1)S(1)} collective-permute-done((bf16[256,128]{1,0:T(8,128)(2,1)S(1)}, bf16[256,128]{1,0:T(8,128)(2,1)S(1)}, u32[]{:S(2)}, u32[]{:S(2)}) %collective-permute-start.9) | collective-permute-done | bytes 65568 | tf_op jit(solution)/shard_map/ppermute | solution.py:98
  44.3 0.0 copy-done.5
  44.3 0.0 copy-done.7
  44.3 0.6 %copy-done.8 = bf16[256,128]{1,0:T(8,128)(2,1)} copy-done((bf16[256,128]{1,0:T(8,128)(2,1)}, bf16[256,128]{1,0:T(8,128)(2,1)S(1)}, u32[]{:S(2)}) %copy-start.8) | copy-done | bytes 65560
  44.9 1.7 %shard_map.77 = (bf16[128,128]{1,0:T(8,128)(2,1)}, bf16[128,128]{1,0:T(8,128)(2,1)}) custom-call(f32[256,128]{1,0:T(8,128)} %copy-done.2, bf16[256,128]{1,0:T(8,128)(2,1)} %copy-done.4, bf16[256,128]{1,0:T(8,128)(2,1)} %copy-done.5, bf16[256,128]{1,0:T(8,128)(2,1)} %copy-done.6, bf16[256,128]{1,0:T(8,128)(2,1)} %copy-done.7, bf16[256,128]{1,0:T(8,128)(2,1)} %copy-done.8), custom_call_target="tpu_custom_call" | custom-call | tf_op jit(solution)/shard_map/pallas_call | solution.py:115
  (12 shorter events, 0.0 us)
Async XLA Ops:
  0.6 0.8 %copy-start.9 = (bf16[128,128]{1,0:T(8,128)(2,1)S(1)}, bf16[128,128]{1,0:T(8,128)(2,1)}, u32[]{:S(2)}) copy-start(bf16[128,128]{1,0:T(8,128)(2,1)} %param.7) | copy-start | bytes 98308
  1.4 11.0 %collective-permute-start.4 = (bf16[256,128]{1,0:T(8,128)(2,1)S(1)}, bf16[256,128]{1,0:T(8,128)(2,1)S(1)}, u32[]{:S(2)}, u32[]{:S(2)}) collective-permute-start(bf16[256,128]{1,0:T(8,128)(2,1)S(1)} %constant_dynamic-update-slice_fusion.refs_2_), channel_id=1, source_target_pairs={{0,20},{4,24},{8,28},{12,0},{16,4},{20,8},{24,12},{28,16},{1,21},{... | collective-permute-start | bytes 196616 | tf_op jit(solution)/shard_map/ppermute | solution.py:98
  6.4 9.5 %collective-permute-start.3 = (bf16[256,128]{1,0:T(8,128)(2,1)S(1)}, bf16[256,128]{1,0:T(8,128)(2,1)S(1)}, u32[]{:S(2)}, u32[]{:S(2)}) collective-permute-start(bf16[256,128]{1,0:T(8,128)(2,1)S(1)} %constant_dynamic-update-slice_fusion.refs_2_), channel_id=1, source_target_pairs={{0,16},{4,20},{8,24},{12,28},{16,0},{20,4},{24,8},{28,12},{1,17},{... | collective-permute-start | bytes 196616 | tf_op jit(solution)/shard_map/ppermute | solution.py:98
  6.8 11.3 %collective-permute-start.2 = (bf16[256,128]{1,0:T(8,128)(2,1)S(1)}, bf16[256,128]{1,0:T(8,128)(2,1)S(1)}, u32[]{:S(2)}, u32[]{:S(2)}) collective-permute-start(bf16[256,128]{1,0:T(8,128)(2,1)S(1)} %constant_dynamic-update-slice_fusion.refs_2_), channel_id=1, source_target_pairs={{0,12},{4,16},{8,20},{12,24},{16,28},{20,0},{24,4},{28,8},{1,13},{... | collective-permute-start | bytes 196616 | tf_op jit(solution)/shard_map/ppermute | solution.py:98
  8.4 9.7 %collective-permute-start.1 = (bf16[256,128]{1,0:T(8,128)(2,1)S(1)}, bf16[256,128]{1,0:T(8,128)(2,1)S(1)}, u32[]{:S(2)}, u32[]{:S(2)}) collective-permute-start(bf16[256,128]{1,0:T(8,128)(2,1)S(1)} %constant_dynamic-update-slice_fusion.refs_2_), channel_id=1, source_target_pairs={{0,8},{4,12},{8,16},{12,20},{16,24},{20,28},{24,0},{28,4},{1,9},{5... | collective-permute-start | bytes 196616 | tf_op jit(solution)/shard_map/ppermute | solution.py:98
  10.9 7.2 %collective-permute-start = (bf16[256,128]{1,0:T(8,128)(2,1)S(1)}, bf16[256,128]{1,0:T(8,128)(2,1)S(1)}, u32[]{:S(2)}, u32[]{:S(2)}) collective-permute-start(bf16[256,128]{1,0:T(8,128)(2,1)S(1)} %constant_dynamic-update-slice_fusion.refs_2_), channel_id=1, source_target_pairs={{0,4},{4,8},{8,12},{12,16},{16,20},{20,24},{24,28},{28,0},{1,5},{5... | collective-permute-start | bytes 196616 | tf_op jit(solution)/shard_map/ppermute | solution.py:98
  18.1 0.7 %copy-start.3 = (s32[16]{0:T(128)S(1)}, s32[16]{0:T(128)}, u32[]{:S(2)}) copy-start(s32[16]{0:T(128)} %lengths.1) | copy-start | bytes 196
  18.8 1.0 %copy-start = (bf16[128,16,128]{2,1,0:T(8,128)(2,1)S(1)}, bf16[128,16,128]{2,1,0:T(8,128)(2,1)}, u32[]{:S(2)}) copy-start(bf16[128,16,128]{2,1,0:T(8,128)(2,1)} %param.5) | copy-start | bytes 1572868
  19.8 1.0 %copy-start.1 = (bf16[128,16,128]{2,1,0:T(8,128)(2,1)S(1)}, bf16[128,16,128]{2,1,0:T(8,128)(2,1)}, u32[]{:S(2)}) copy-start(bf16[128,16,128]{2,1,0:T(8,128)(2,1)} %param.8) | copy-start | bytes 1572868
  31.0 0.6 %copy-start.2 = (f32[256,128]{1,0:T(8,128)}, f32[256,128]{1,0:T(8,128)S(1)}, u32[]{:S(2)}) copy-start(f32[256,128]{1,0:T(8,128)S(1)} %get-tuple-element.13.refs_0_) | copy-start | bytes 393220
  31.6 5.4 %collective-permute-start.5 = (bf16[256,128]{1,0:T(8,128)(2,1)S(1)}, bf16[256,128]{1,0:T(8,128)(2,1)S(1)}, u32[]{:S(2)}, u32[]{:S(2)}) collective-permute-start(bf16[256,128]{1,0:T(8,128)(2,1)S(1)} %get-tuple-element.14), channel_id=1, source_target_pairs={{0,28},{4,0},{8,4},{12,8},{16,12},{20,16},{24,20},{28,24},{1,29},{... | collective-permute-start | bytes 196616 | tf_op jit(solution)/shard_map/ppermute | solution.py:98
  32.0 5.0 %collective-permute-start.6 = (bf16[256,128]{1,0:T(8,128)(2,1)S(1)}, bf16[256,128]{1,0:T(8,128)(2,1)S(1)}, u32[]{:S(2)}, u32[]{:S(2)}) collective-permute-start(bf16[256,128]{1,0:T(8,128)(2,1)S(1)} %get-tuple-element.15), channel_id=1, source_target_pairs={{0,24},{4,28},{8,0},{12,4},{16,8},{20,12},{24,16},{28,20},{1,25},{... | collective-permute-start | bytes 196616 | tf_op jit(solution)/shard_map/ppermute | solution.py:98
  34.1 5.4 %collective-permute-start.7 = (bf16[256,128]{1,0:T(8,128)(2,1)S(1)}, bf16[256,128]{1,0:T(8,128)(2,1)S(1)}, u32[]{:S(2)}, u32[]{:S(2)}) collective-permute-start(bf16[256,128]{1,0:T(8,128)(2,1)S(1)} %get-tuple-element.16), channel_id=1, source_target_pairs={{0,20},{4,24},{8,28},{12,0},{16,4},{20,8},{24,12},{28,16},{1,21},{... | collective-permute-start | bytes 196616 | tf_op jit(solution)/shard_map/ppermute | solution.py:98
  34.9 8.7 %collective-permute-start.8 = (bf16[256,128]{1,0:T(8,128)(2,1)S(1)}, bf16[256,128]{1,0:T(8,128)(2,1)S(1)}, u32[]{:S(2)}, u32[]{:S(2)}) collective-permute-start(bf16[256,128]{1,0:T(8,128)(2,1)S(1)} %get-tuple-element.17), channel_id=1, source_target_pairs={{0,16},{4,20},{8,24},{12,28},{16,0},{20,4},{24,8},{28,12},{1,17},{... | collective-permute-start | bytes 196616 | tf_op jit(solution)/shard_map/ppermute | solution.py:98
  36.6 7.6 %collective-permute-start.9 = (bf16[256,128]{1,0:T(8,128)(2,1)S(1)}, bf16[256,128]{1,0:T(8,128)(2,1)S(1)}, u32[]{:S(2)}, u32[]{:S(2)}) collective-permute-start(bf16[256,128]{1,0:T(8,128)(2,1)S(1)} %get-tuple-element.18), channel_id=1, source_target_pairs={{0,12},{4,16},{8,20},{12,24},{16,28},{20,0},{24,4},{28,8},{1,13},{... | collective-permute-start | bytes 196616 | tf_op jit(solution)/shard_map/ppermute | solution.py:98
  37.0 7.2 %copy-start.4 = (bf16[256,128]{1,0:T(8,128)(2,1)}, bf16[256,128]{1,0:T(8,128)(2,1)S(1)}, u32[]{:S(2)}) copy-start(bf16[256,128]{1,0:T(8,128)(2,1)S(1)} %collective-permute-done.5.refs_1_) | copy-start | bytes 196612
  37.0 7.2 %copy-start.5 = (bf16[256,128]{1,0:T(8,128)(2,1)}, bf16[256,128]{1,0:T(8,128)(2,1)S(1)}, u32[]{:S(2)}) copy-start(bf16[256,128]{1,0:T(8,128)(2,1)S(1)} %collective-permute-done.6.refs_2_) | copy-start | bytes 196612
  39.5 4.8 %copy-start.6 = (bf16[256,128]{1,0:T(8,128)(2,1)}, bf16[256,128]{1,0:T(8,128)(2,1)S(1)}, u32[]{:S(2)}) copy-start(bf16[256,128]{1,0:T(8,128)(2,1)S(1)} %collective-permute-done.7.refs_3_) | copy-start | bytes 196612
  43.6 0.7 %copy-start.7 = (bf16[256,128]{1,0:T(8,128)(2,1)}, bf16[256,128]{1,0:T(8,128)(2,1)S(1)}, u32[]{:S(2)}) copy-start(bf16[256,128]{1,0:T(8,128)(2,1)S(1)} %collective-permute-done.8.refs_4_) | copy-start | bytes 196612
  44.2 0.6 %copy-start.8 = (bf16[256,128]{1,0:T(8,128)(2,1)}, bf16[256,128]{1,0:T(8,128)(2,1)S(1)}, u32[]{:S(2)}) copy-start(bf16[256,128]{1,0:T(8,128)(2,1)S(1)} %collective-permute-done.9.refs_5_) | copy-start | bytes 196612
where the time goes:
time: 46.9 us; the launch traced here: 46.6 us
  starting transfers between devices  16.4 us (35%)
  waiting for transfers between devices  12.9 us (28%)
  Pallas kernels  11.8 us (25%)
  local copies, waits for them, and re-layouts  4.77 us (10%)
  between operations  0.68 us (1%)
    ppermute x10, starting transfers between devices, turn(): return lax.ppermute(x, 'ctx', [(i, (i + by) % count) for i in range(count)])  16.4 us
    ppermute x10, waiting for transfers between devices, turn(): return lax.ppermute(x, 'ctx', [(i, (i + by) % count) for i in range(count)])  12.9 us
    pallas_call x1, Pallas kernels, on_device(): pl.pallas_call(functools.partial(attend, back, heads), out_shape=[jax.Sha...  10.1 us
    unnamed x21, local copies, waits for them, and re-layouts  4.76 us
    pallas_call x1, Pallas kernels, on_device(): pl.pallas_call(combine, out_shape=[jax.ShapeDtypeStruct((rows, width), jn...  1.69 us
  transfers between devices with their start and end apart: 10, of which 5 were waited for; matrix products, arithmetic and copies ran while one was open for 0% of the time, Pallas kernels for 0%

commit v1 on v0

v1 whole, which is shorter than its diff:
```python
import functools
import math

import jax
import jax.numpy as jnp
from jax import lax
from jax.experimental import pallas as pl
from jax.experimental.pallas import tpu as pltpu
from jax.sharding import PartitionSpec as P

NT = (((1,), (1,)), ((), ()))
TILE = 256
EARLY = 2
F32, BF16 = jnp.float32, jnp.bfloat16
VMEM = pl.BlockSpec(memory_space=pltpu.VMEM)
SMEM = pl.BlockSpec(memory_space=pltpu.SMEM)
FAR = pl.BlockSpec(memory_space=pltpu.HBM)


def shape(*dims, dtype=BF16):
    return jax.ShapeDtypeStruct(dims, dtype)


def call(kernel, outs, scratch=(), mib=8, flops=0, far=()):
    def run(*args):
        in_specs = [FAR if n in far else SMEM if a.ndim == 1 else VMEM for n, a in enumerate(args)]
        args = [pltpu.with_memory_space_constraint(a, pltpu.HBM) if n in far else a for n, a in enumerate(args)]
        return pl.pallas_call(
            kernel,
            out_shape=outs,
            in_specs=in_specs,
            out_specs=[VMEM] * len(outs),
            scratch_shapes=scratch,
            compiler_params=pltpu.CompilerParams(vmem_limit_bytes=mib * 2**20),
            cost_estimate=pl.CostEstimate(flops=flops, bytes_accessed=2**20, transcendentals=0),
        )(*args)

    return run


def doc_begin(pos, lengths):
    low, end = jnp.zeros_like(pos), jnp.int32(0)
    for n in range(lengths.shape[0]):
        end = end + lengths[n]
        low = jnp.where(end <= pos, jnp.maximum(low, end), low)
    return low


def pack_kernel(k_far, v_far, pair_ref, sems):
    block = k_far.shape[0]
    copies = [
        pltpu.make_async_copy(k_far, pair_ref.at[pl.ds(0, block)], sems.at[0]),
        pltpu.make_async_copy(v_far, pair_ref.at[pl.ds(block, block)], sems.at[1]),
    ]
    for c in copies:
        c.start()
    for c in copies:
        c.wait()


def masked_scores(pair_ref, q, low, row, shift):
    block = pair_ref.shape[0] // 2
    key = lax.broadcasted_iota(jnp.int32, (block, q.shape[0]), 0).astype(F32)
    s = lax.dot_general(pair_ref[:block, :], q, NT, preferred_element_type=F32)
    allowed = key >= low + float(shift * block)
    if shift == 0:
        allowed = allowed & (key <= row)
    return jnp.where(allowed, s, -1e30)


def early_kernel(shifts, heads, to_exp2, start, lengths_far, q_far, g_far, *refs):
    pairs = refs[: len(shifts)]
    q_ref, g_ref, e_ref, gp_ref, stat_ref, lengths, q_sems, g_sems, len_sem = refs[len(shifts) :]
    block = pairs[0].shape[0] // 2
    first = start[0]
    tiles = q_ref.shape[0] // TILE
    len_copy = pltpu.make_async_copy(lengths_far, lengths, len_sem)
    len_copy.start()
    copies = []
    for index in range(tiles):
        at = pl.ds(index * TILE, TILE)
        copies.append(
            (
                pltpu.make_async_copy(q_far.at[at], q_ref.at[at], q_sems.at[index]),
                pltpu.make_async_copy(g_far.at[at], g_ref.at[at], g_sems.at[index]),
            )
        )
        for c in copies[-1]:
            c.start()
    len_copy.wait()
    for index in range(tiles):
        at = pl.ds(index * TILE, TILE)
        row = lax.div(lax.broadcasted_iota(jnp.int32, (1, TILE), 1) + index * TILE, heads)
        low = (doc_begin(first + row, lengths) - first).astype(F32)
        row = row.astype(F32)
        for c in copies[index]:
            c.wait()
        q, g = q_ref[at, :], g_ref[at, :]
        scores, top = [], None
        for n, shift in enumerate(shifts):
            s = masked_scores(pairs[n], q, low, row, shift)
            high = jnp.max(s, axis=0, keepdims=True)
            top = high if top is None else jnp.maximum(top, high)
            scores.append(s)
        total, weighted = 0.0, 0.0
        for n in range(len(shifts)):
            e = jnp.exp2((scores[n] - top) * to_exp2)
            gp = lax.dot_general(pairs[n][block:, :], g, NT, preferred_element_type=F32)
            total = total + jnp.sum(e, axis=0, keepdims=True)
            weighted = weighted + jnp.sum(e * gp, axis=0, keepdims=True)
            e_ref[n * block : (n + 1) * block, at] = e
            gp_ref[n * block : (n + 1) * block, at] = gp
        stat_ref[0:1, at] = top
        stat_ref[1:2, at] = total
        stat_ref[2:3, at] = weighted
        stat_ref[3:4, at] = low


def main_kernel(early, late, scale, to_exp2, *refs):
    q_ref, g_ref, e_ref, gp_ref, stat_ref = refs[:5]
    pairs = refs[5 : 5 + len(late)]
    p_own, ds_ref = refs[5 + len(late) : 7 + len(late)]
    sent = refs[7 + len(late) : -2]
    p_ref, acc = refs[-2:]
    back = len(sent)
    block = pairs[0].shape[0] // 2
    tiles = q_ref.shape[0] // TILE

    def keep(shift, at, p, ds):
        if shift == 0:
            p_own[:, at] = p.astype(BF16)
        else:
            p_ref[(shift - 1) * block : shift * block, at] = p.astype(BF16)
        ds_ref[shift * block : (shift + 1) * block, at] = ds.astype(BF16)

    def probabilities(index):
        at = pl.ds(index * TILE, TILE)
        q, g = q_ref[at, :], g_ref[at, :]
        early_top, low = stat_ref[0:1, at], stat_ref[3:4, at]
        top, scores = early_top, []
        for n, shift in enumerate(late):
            s = masked_scores(pairs[n], q, low, None, shift)
            top = jnp.maximum(top, jnp.max(s, axis=0, keepdims=True))
            scores.append(s)
        factor = jnp.exp2((early_top - top) * to_exp2)
        total, weighted = stat_ref[1:2, at] * factor, stat_ref[2:3, at] * factor
        exps, grads = [], []
        for n in range(len(late)):
            e = jnp.exp2((scores[n] - top) * to_exp2)
            gp = lax.dot_general(pairs[n][block:, :], g, NT, preferred_element_type=F32)
            total = total + jnp.sum(e, axis=0, keepdims=True)
            weighted = weighted + jnp.sum(e * gp, axis=0, keepdims=True)
            exps.append(e)
            grads.append(gp)
        inverse = 1.0 / total
        delta = weighted * inverse
        for n, shift in enumerate(early):
            part = slice(n * block, (n + 1) * block)
            p = e_ref[part, at] * (factor * inverse)
            keep(shift, at, p, p * (gp_ref[part, at] - delta))
        for n, shift in enumerate(late):
            p = exps[n] * inverse
            keep(shift, at, p, p * (grads[n] - delta))

    def sums(index):
        at = pl.ds(index * TILE, TILE)
        dk = jnp.dot(ds_ref[block:, at], q_ref[at, :], preferred_element_type=F32)
        dv = jnp.dot(p_ref[:, at], g_ref[at, :], preferred_element_type=F32)
        if index == 0:
            acc[0], acc[1] = dk, dv
        else:
            acc[0] += dk
            acc[1] += dv

    for index in range(tiles):
        probabilities(index)
        if index:
            sums(index - 1)
    sums(tiles - 1)
    for b in range(back):
        at = slice(b * block, (b + 1) * block)
        sent[b][:block, :] = (acc[0, at, :] * scale).astype(BF16)
        sent[b][block:, :] = acc[1, at, :].astype(BF16)


def rest_kernel(back, scale, *refs):
    q_ref, g_ref, p_own, ds_ref = refs[:4]
    pairs, (dq_ref, own_ref, k_ref) = refs[4 : 5 + back], refs[5 + back :]
    block = pairs[0].shape[0] // 2
    for b in range(back + 1):
        k_ref[:, b * block : (b + 1) * block] = pairs[b][:block, :].T
    own_ref[:block, :] = jnp.dot(ds_ref[:block, :], q_ref[...], preferred_element_type=F32) * scale
    own_ref[block:, :] = jnp.dot(p_own[...], g_ref[...], preferred_element_type=F32)
    dq = jnp.dot(k_ref[...], ds_ref[...], preferred_element_type=F32) * scale
    dq_ref[...] = dq.T.astype(BF16)


def combine(own, *refs):
    rest, (dk, dv) = refs[:-2], refs[-2:]
    block = dk.shape[0]
    total = own[...]
    for r in rest:
        total = total + r[...].astype(F32)
    dk[...] = total[:block].astype(BF16)
    dv[...] = total[block:].astype(BF16)


def whole_kernel(back, heads, scale, to_exp2, lengths, start, *refs):
    q_ref, g_ref = refs[0], refs[1]
    pairs = refs[2 : 3 + back]
    dq_ref, own_ref = refs[3 + back], refs[4 + back]
    sent = refs[5 + back : 5 + 2 * back]
    acc = refs[5 + 2 * back]
    block = pairs[0].shape[0] // 2
    first = start[0]

    def tile(index, carry):
        at = pl.ds(pl.multiple_of(index * TILE, TILE), TILE)
        q, g = q_ref[at, :], g_ref[at, :]
        row = lax.div(lax.broadcasted_iota(jnp.int32, (1, TILE), 1) + index * TILE, heads)
        low = doc_begin(first + row, lengths) - first
        key = lax.broadcasted_iota(jnp.int32, (block, TILE), 0)
        scores, top = [], None
        for b in range(back + 1):
            s = lax.dot_general(pairs[b][:block, :], q, NT, preferred_element_type=F32)
            allowed = (key >= low) & (key <= row) if b == 0 else key >= low + b * block
            s = jnp.where(allowed, s, -1e30)
            high = jnp.max(s, axis=0, keepdims=True)
            top = high if top is None else jnp.maximum(top, high)
            scores.append(s)
        total, weighted, exps, grads = 0.0, 0.0, [], []
        for b in range(back + 1):
            e = jnp.exp2((scores[b] - top) * to_exp2)
            gp = lax.dot_general(pairs[b][block:, :], g, NT, preferred_element_type=F32)
            total = total + jnp.sum(e, axis=0, keepdims=True)
            weighted = weighted + jnp.sum(e * gp, axis=0, keepdims=True)
            exps.append(e)
            grads.append(gp)
        inverse = 1.0 / total
        delta = weighted * inverse
        dq = None
        for b in range(back + 1):
            p = exps[b] * inverse
            ds = (p * (grads[b] - delta)).astype(BF16)
            acc[b, :block, :] += jnp.dot(ds, q, preferred_element_type=F32)
            acc[b, block:, :] += jnp.dot(p.astype(BF16), g, preferred_element_type=F32)
            part = lax.dot_general(
                ds, pairs[b][:block, :], (((0,), (0,)), ((), ())), preferred_element_type=F32
            )
            dq = part if dq is None else dq + part
        dq_ref[at, :] = (dq * scale).astype(BF16)
        return carry

    acc[...] = jnp.zeros_like(acc)
    lax.fori_loop(0, q_ref.shape[0] // TILE, tile, 0)
    for b in range(back + 1):
        out = own_ref if b == 0 else sent[b - 1]
        out[:block, :] = (acc[b, :block, :] * scale).astype(out.dtype)
        out[block:, :] = acc[b, block:, :].astype(out.dtype)


def on_device(queries, keys, values, grad_out, lengths):
    rows, heads, width = queries.shape
    count = lax.axis_size("ctx")
    longest = rows * count // 2 + rows
    back = min(count - 1, -(-(longest - 1) // rows))
    start = (lax.axis_index("ctx") * rows).astype(jnp.int32).reshape(1)
    scale = 1.0 / math.sqrt(width)
    to_exp2 = scale * math.log2(math.e)
    q, g = queries.reshape(-1, width), grad_out.reshape(-1, width)
    flat = rows * heads

    def turn(x, by):
        return lax.ppermute(x, "ctx", [(i, (i + by) % count) for i in range(count)])

    pair = call(pack_kernel, [shape(2 * rows, width)], [pltpu.SemaphoreType.DMA((2,))], mib=1, far=(0, 1))(
        keys, values
    )[0]
    others = [turn(pair, b) for b in range(1, back + 1)]
    partial = shape(2 * rows, width)
    if back > 7:
        dq, own, *sent = call(
            functools.partial(whole_kernel, back, heads, scale, to_exp2),
            [shape(flat, width), shape(2 * rows, width, dtype=F32)] + [partial] * back,
            [pltpu.VMEM((back + 1, 2 * rows, width), F32)],
            mib=48,
        )(lengths, start, q, g, pair, *others)
        returned = [turn(sent[b - 1], -b) for b in range(1, back + 1)]
    else:
        early = (0,) + tuple(range(back, back - EARLY, -1))
        late = tuple(range(1, back + 1 - EARLY))
        tall = len(early) * rows
        tiles = flat // TILE
        q, g, e, gp, stat = call(
            functools.partial(early_kernel, early, heads, to_exp2),
            [
                shape(flat, width),
                shape(flat, width),
                shape(tall, flat, dtype=F32),
                shape(tall, flat, dtype=F32),
                shape(8, flat, dtype=F32),
            ],
            [
                pltpu.SMEM(lengths.shape, jnp.int32),
                pltpu.SemaphoreType.DMA((tiles,)),
                pltpu.SemaphoreType.DMA((tiles,)),
                pltpu.SemaphoreType.DMA,
            ],
            flops=2**29,
            far=(1, 2, 3),
        )(start, lengths, q, g, *([pair, *others][shift] for shift in early))
        p_own, ds, *sent = call(
            functools.partial(main_kernel, early, late, scale, to_exp2),
            [shape(rows, flat), shape((back + 1) * rows, flat)] + [partial] * back,
            [pltpu.VMEM((back * rows, flat), BF16), pltpu.VMEM((2, back * rows, width), F32)],
            mib=16,
            flops=2**31,
        )(q, g, e, gp, stat, *(others[shift - 1] for shift in late))
        returned = [turn(sent[b - 1], -b) for b in range(1, back + 1)]
        dq, own = call(
            functools.partial(rest_kernel, back, scale),
            [shape(flat, width), shape(2 * rows, width, dtype=F32)],
            [pltpu.VMEM((width, (back + 1) * rows), BF16)],
            flops=2**29,
        )(q, g, p_own, ds, pair, *others)
    dk, dv = call(combine, [shape(rows, width)] * 2, mib=4)(own, *returned)
    return dq.reshape(queries.shape), dk, dv


def solution(mesh):
    return jax.shard_map(
        on_device,
        mesh=mesh,
        in_specs=(
            P("ctx", "grp", None),
            P("ctx", "grp"),
            P("ctx", "grp"),
            P("ctx", "grp", None),
            P(),
        ),
        out_specs=(P("ctx", "grp", None), P("ctx", "grp"), P("ctx", "grp")),
        check_vma=False,
    )
```

time: 46.9 us -> 35.7 us (0.76)
  waiting for transfers between devices: 12.9 us -> 4.03 us
  local copies, waits for them, and re-layouts: 4.77 us -> 0 us
  starting transfers between devices: 16.4 us -> 20.5 us
  Pallas kernels: 11.8 us -> 10.3 us
    ppermute x10, waiting for transfers between devices: 12.9 us -> 4.03 us  [turn(): return lax.ppermute(x, 'ctx', [(i, (i + by) % count) for i in range(count)])]
    unnamed x21 -> x0, local copies, waits for them, and re-layouts: 4.76 us -> none
    ppermute x10, starting transfers between devices: 16.4 us -> 20.5 us  [turn(): return lax.ppermute(x, 'ctx', [(i, (i + by) % count) for i in range(count)])]
    pallas_call x2 -> x5, Pallas kernels: 11.8 us -> 10.3 us  [run(): pl.pallas_call(kernel, out_shape=outs, in_specs=in_specs, out_specs=[VMEM...]
  transfers between devices with their start and end apart: 10 -> 10, of which waited for: 5 -> 3; matrix products, arithmetic and copies ran while one was open for 0% -> 0% of each run, Pallas kernels for 0% -> 16%
where the time goes in v1:
time: 35.7 us; the launch traced here: 35.5 us
  starting transfers between devices  20.5 us (57%)
  Pallas kernels  10.3 us (29%)
  waiting for transfers between devices  4.03 us (11%)
  between operations  0.66 us (2%)
    ppermute x10, starting transfers between devices, turn(): return lax.ppermute(x, 'ctx', [(i, (i + by) % count) for i in range(count)])  20.5 us
    pallas_call x5, Pallas kernels, run(): pl.pallas_call(kernel, out_shape=outs, in_specs=in_specs, out_specs=[VMEM...  10.3 us
    ppermute x10, waiting for transfers between devices, turn(): return lax.ppermute(x, 'ctx', [(i, (i + by) % count) for i in range(count)])  4.03 us
  transfers between devices with their start and end apart: 10, of which 3 were waited for; matrix products, arithmetic and copies ran while one was open for 0% of the time, Pallas kernels for 16%

profile of v1, /device:TPU:0, one launch (start us, length us, event | category | flops | bytes accessed | tf_op | source)
XLA Modules:
  0.0 35.5 jit_solution(11647859940587478843)
XLA Ops:
  0.6 0.8 %shard_map.76.refs_0_.refs_4_ = bf16[256,128]{1,0:T(8,128)(2,1)S(1)} custom-call(bf16[128,128]{1,0:T(8,128)(2,1)} %k_far.1, bf16[128,128]{1,0:T(8,128)(2,1)} %v_far.1), custom_call_target="tpu_custom_call" | custom-call | bytes 1048576 | tf_op jit(solution)/shard_map/pallas_call | solution.py:28
  1.4 4.1 %collective-permute-start.1 = (bf16[256,128]{1,0:T(8,128)(2,1)S(1)}, bf16[256,128]{1,0:T(8,128)(2,1)S(1)}, u32[]{:S(2)}, u32[]{:S(2)}) collective-permute-start(bf16[256,128]{1,0:T(8,128)(2,1)S(1)} %shard_map.76.refs_0_.refs_4_), channel_id=1, source_target_pairs={{0,16},{4,20},{8,24},{12,28},{16,0},{20,4},{24,8},{28,12},{1,17},{... | collective-permute-start | bytes 196616 | tf_op jit(solution)/shard_map/ppermute | solution.py:274
  5.5 1.3 %collective-permute-start = (bf16[256,128]{1,0:T(8,128)(2,1)S(1)}, bf16[256,128]{1,0:T(8,128)(2,1)S(1)}, u32[]{:S(2)}, u32[]{:S(2)}) collective-permute-start(bf16[256,128]{1,0:T(8,128)(2,1)S(1)} %shard_map.76.refs_0_.refs_4_), channel_id=1, source_target_pairs={{0,20},{4,24},{8,28},{12,0},{16,4},{20,8},{24,12},{28,16},{1,21},{... | collective-permute-start | bytes 196616 | tf_op jit(solution)/shard_map/ppermute | solution.py:274
  6.8 1.7 %collective-permute-start.4 = (bf16[256,128]{1,0:T(8,128)(2,1)S(1)}, bf16[256,128]{1,0:T(8,128)(2,1)S(1)}, u32[]{:S(2)}, u32[]{:S(2)}) collective-permute-start(bf16[256,128]{1,0:T(8,128)(2,1)S(1)} %shard_map.76.refs_0_.refs_4_), channel_id=1, source_target_pairs={{0,12},{4,16},{8,20},{12,24},{16,28},{20,0},{24,4},{28,8},{1,13},{... | collective-permute-start | bytes 196616 | tf_op jit(solution)/shard_map/ppermute | solution.py:274
  8.5 1.6 %collective-permute-start.3 = (bf16[256,128]{1,0:T(8,128)(2,1)S(1)}, bf16[256,128]{1,0:T(8,128)(2,1)S(1)}, u32[]{:S(2)}, u32[]{:S(2)}) collective-permute-start(bf16[256,128]{1,0:T(8,128)(2,1)S(1)} %shard_map.76.refs_0_.refs_4_), channel_id=1, source_target_pairs={{0,8},{4,12},{8,16},{12,20},{16,24},{20,28},{24,0},{28,4},{1,9},{5... | collective-permute-start | bytes 196616 | tf_op jit(solution)/shard_map/ppermute | solution.py:274
  10.0 2.4 %collective-permute-start.2 = (bf16[256,128]{1,0:T(8,128)(2,1)S(1)}, bf16[256,128]{1,0:T(8,128)(2,1)S(1)}, u32[]{:S(2)}, u32[]{:S(2)}) collective-permute-start(bf16[256,128]{1,0:T(8,128)(2,1)S(1)} %shard_map.76.refs_0_.refs_4_), channel_id=1, source_target_pairs={{0,4},{4,8},{8,12},{12,16},{16,20},{20,24},{24,28},{28,0},{1,5},{5... | collective-permute-start | bytes 196616 | tf_op jit(solution)/shard_map/ppermute | solution.py:274
  12.4 0.0 collective-permute-done.1.refs_2_.refs_8_
  12.4 0.0 collective-permute-done.refs_1_.refs_9_
  12.4 3.9 %shard_map.77 = (bf16[2048,128]{1,0:T(8,128)(2,1)S(1)}, bf16[2048,128]{1,0:T(8,128)(2,1)S(1)}, f32[384,2048]{1,0:T(8,128)S(1)}, f32[384,2048]{1,0:T(8,128)S(1)}, f32[8,2048]{1,0:T(8,128)S(1)}) custom-call(s32[1]{0:T(128)} %bitcast.start, s32[16]{0:T(128)} %lengths_far.1, bf16[2048,128]{1,0:T(8,128)(2,1)} %bitcast.4, bf16[2048,128]{1,0:T(8,128)(2,1)} %bitcast.5, ...), custom_call_target="tpu_custom_call" | custom-call | flops 536870912 | bytes 1048576 | tf_op jit(solution)/shard_map/pallas_call | solution.py:28
  16.3 1.0 %collective-permute-done.4.refs_7_ = bf16[256,128]{1,0:T(8,128)(2,1)S(1)} collective-permute-done((bf16[256,128]{1,0:T(8,128)(2,1)S(1)}, bf16[256,128]{1,0:T(8,128)(2,1)S(1)}, u32[]{:S(2)}, u32[]{:S(2)}) %collective-permute-start.4) | collective-permute-done | bytes 65568 | tf_op jit(solution)/shard_map/ppermute | solution.py:274
  17.3 0.0 collective-permute-done.3.refs_6_
  17.3 0.0 collective-permute-done.2.refs_5_
  17.3 3.3 %shard_map.78 = (bf16[128,2048]{1,0:T(8,128)(2,1)S(1)}, bf16[768,2048]{1,0:T(8,128)(2,1)S(1)}, bf16[256,128]{1,0:T(8,128)(2,1)S(1)}, bf16[256,128]{1,0:T(8,128)(...) custom-call(bf16[2048,128]{1,0:T(8,128)(2,1)S(1)} %get-tuple-element.19.refs_0_, ...), custom_call_target="tpu_custom_call" | custom-call | flops 2147483648 | bytes 1048576 | tf_op jit(solution)/shard_map/pallas_call | solution.py:28
  20.7 3.2 %collective-permute-start.5 = (bf16[256,128]{1,0:T(8,128)(2,1)S(1)}, bf16[256,128]{1,0:T(8,128)(2,1)S(1)}, u32[]{:S(2)}, u32[]{:S(2)}) collective-permute-start(bf16[256,128]{1,0:T(8,128)(2,1)S(1)} %get-tuple-element.28), channel_id=1, source_target_pairs={{0,28},{4,0},{8,4},{12,8},{16,12},{20,16},{24,20},{28,24},{1,29},{... | collective-permute-start | bytes 196616 | tf_op jit(solution)/shard_map/ppermute | solution.py:274
  23.9 0.0 collective-permute-start.6
  23.9 0.6 %collective-permute-start.7 = (bf16[256,128]{1,0:T(8,128)(2,1)S(1)}, bf16[256,128]{1,0:T(8,128)(2,1)S(1)}, u32[]{:S(2)}, u32[]{:S(2)}) collective-permute-start(bf16[256,128]{1,0:T(8,128)(2,1)S(1)} %get-tuple-element.30), channel_id=1, source_target_pairs={{0,20},{4,24},{8,28},{12,0},{16,4},{20,8},{24,12},{28,16},{1,21},{... | collective-permute-start | bytes 196616 | tf_op jit(solution)/shard_map/ppermute | solution.py:274
  24.5 2.7 %collective-permute-start.8 = (bf16[256,128]{1,0:T(8,128)(2,1)S(1)}, bf16[256,128]{1,0:T(8,128)(2,1)S(1)}, u32[]{:S(2)}, u32[]{:S(2)}) collective-permute-start(bf16[256,128]{1,0:T(8,128)(2,1)S(1)} %get-tuple-element.31), channel_id=1, source_target_pairs={{0,16},{4,20},{8,24},{12,28},{16,0},{20,4},{24,8},{28,12},{1,17},{... | collective-permute-start | bytes 196616 | tf_op jit(solution)/shard_map/ppermute | solution.py:274
  27.2 2.9 %collective-permute-start.9 = (bf16[256,128]{1,0:T(8,128)(2,1)S(1)}, bf16[256,128]{1,0:T(8,128)(2,1)S(1)}, u32[]{:S(2)}, u32[]{:S(2)}) collective-permute-start(bf16[256,128]{1,0:T(8,128)(2,1)S(1)} %get-tuple-element.32), channel_id=1, source_target_pairs={{0,12},{4,16},{8,20},{12,24},{16,28},{20,0},{24,4},{28,8},{1,13},{... | collective-permute-start | bytes 196616 | tf_op jit(solution)/shard_map/ppermute | solution.py:274
  30.1 1.7 %shard_map.79 = (bf16[2048,128]{1,0:T(8,128)(2,1)}, f32[256,128]{1,0:T(8,128)S(1)}) custom-call(bf16[2048,128]{1,0:T(8,128)(2,1)S(1)} %get-tuple-element.19.refs_0_, bf16[2048,128]{1,0:T(8,128)(2,1)S(1)} %get-tuple-element.20.refs_1_, bf16[128,2048]{1,0:T(8,128)(2,1)S(1)} %get-tuple-element.24.refs_2_, bf16[768,2048]{1,0:T(8,128)(2,1)S(1)} %get-tuple-element.25.refs_3_, ...), custom_call_target="tpu_custom_call" | custom-call | flops 536870912 | bytes 1048576 | tf_op jit(solution)/shard_map/pallas_call | solution.py:28
  31.8 0.0 collective-permute-done.5.refs_0_
  31.8 0.0 collective-permute-done.6.refs_1_
  31.8 0.0 collective-permute-done.7.refs_2_
  31.9 1.5 %collective-permute-done.8.refs_3_ = bf16[256,128]{1,0:T(8,128)(2,1)S(1)} collective-permute-done((bf16[256,128]{1,0:T(8,128)(2,1)S(1)}, bf16[256,128]{1,0:T(8,128)(2,1)S(1)}, u32[]{:S(2)}, u32[]{:S(2)}) %collective-permute-start.8) | collective-permute-done | bytes 65568 | tf_op jit(solution)/shard_map/ppermute | solution.py:274
  33.4 1.5 %collective-permute-done.9.refs_4_ = bf16[256,128]{1,0:T(8,128)(2,1)S(1)} collective-permute-done((bf16[256,128]{1,0:T(8,128)(2,1)S(1)}, bf16[256,128]{1,0:T(8,128)(2,1)S(1)}, u32[]{:S(2)}, u32[]{:S(2)}) %collective-permute-start.9) | collective-permute-done | bytes 65568 | tf_op jit(solution)/shard_map/ppermute | solution.py:274
  34.8 0.7 %shard_map.80 = (bf16[128,128]{1,0:T(8,128)(2,1)}, bf16[128,128]{1,0:T(8,128)(2,1)}) custom-call(f32[256,128]{1,0:T(8,128)S(1)} %get-tuple-element.27.own, bf16[256,128]{1,0:T(8,128)(2,1)S(1)} %collective-permute-done.5.refs_0_, bf16[256,128]{1,0:T(8,128)(2,1)S(1)} %collective-permute-done.6.refs_1_, bf16[256,128]{1,0:T(8,128)(2,1)S(1)} %collective-permute-done.7.refs_2_, ...), custom_call_target="tpu_custom_call" | custom-call | bytes 1048576 | tf_op jit(solution)/shard_map/pallas_call | solution.py:28
Async XLA Ops:
  1.4 11.0 %collective-permute-start.1 = (bf16[256,128]{1,0:T(8,128)(2,1)S(1)}, bf16[256,128]{1,0:T(8,128)(2,1)S(1)}, u32[]{:S(2)}, u32[]{:S(2)}) collective-permute-start(bf16[256,128]{1,0:T(8,128)(2,1)S(1)} %shard_map.76.refs_0_.refs_4_), channel_id=1, source_target_pairs={{0,16},{4,20},{8,24},{12,28},{16,0},{20,4},{24,8},{28,12},{1,17},{... | collective-permute-start | bytes 196616 | tf_op jit(solution)/shard_map/ppermute | solution.py:274
  5.5 6.9 %collective-permute-start = (bf16[256,128]{1,0:T(8,128)(2,1)S(1)}, bf16[256,128]{1,0:T(8,128)(2,1)S(1)}, u32[]{:S(2)}, u32[]{:S(2)}) collective-permute-start(bf16[256,128]{1,0:T(8,128)(2,1)S(1)} %shard_map.76.refs_0_.refs_4_), channel_id=1, source_target_pairs={{0,20},{4,24},{8,28},{12,0},{16,4},{20,8},{24,12},{28,16},{1,21},{... | collective-permute-start | bytes 196616 | tf_op jit(solution)/shard_map/ppermute | solution.py:274
  6.8 10.5 %collective-permute-start.4 = (bf16[256,128]{1,0:T(8,128)(2,1)S(1)}, bf16[256,128]{1,0:T(8,128)(2,1)S(1)}, u32[]{:S(2)}, u32[]{:S(2)}) collective-permute-start(bf16[256,128]{1,0:T(8,128)(2,1)S(1)} %shard_map.76.refs_0_.refs_4_), channel_id=1, source_target_pairs={{0,12},{4,16},{8,20},{12,24},{16,28},{20,0},{24,4},{28,8},{1,13},{... | collective-permute-start | bytes 196616 | tf_op jit(solution)/shard_map/ppermute | solution.py:274
  8.5 8.9 %collective-permute-start.3 = (bf16[256,128]{1,0:T(8,128)(2,1)S(1)}, bf16[256,128]{1,0:T(8,128)(2,1)S(1)}, u32[]{:S(2)}, u32[]{:S(2)}) collective-permute-start(bf16[256,128]{1,0:T(8,128)(2,1)S(1)} %shard_map.76.refs_0_.refs_4_), channel_id=1, source_target_pairs={{0,8},{4,12},{8,16},{12,20},{16,24},{20,28},{24,0},{28,4},{1,9},{5... | collective-permute-start | bytes 196616 | tf_op jit(solution)/shard_map/ppermute | solution.py:274
  10.0 7.3 %collective-permute-start.2 = (bf16[256,128]{1,0:T(8,128)(2,1)S(1)}, bf16[256,128]{1,0:T(8,128)(2,1)S(1)}, u32[]{:S(2)}, u32[]{:S(2)}) collective-permute-start(bf16[256,128]{1,0:T(8,128)(2,1)S(1)} %shard_map.76.refs_0_.refs_4_), channel_id=1, source_target_pairs={{0,4},{4,8},{8,12},{12,16},{16,20},{20,24},{24,28},{28,0},{1,5},{5... | collective-permute-start | bytes 196616 | tf_op jit(solution)/shard_map/ppermute | solution.py:274
  20.7 11.2 %collective-permute-start.5 = (bf16[256,128]{1,0:T(8,128)(2,1)S(1)}, bf16[256,128]{1,0:T(8,128)(2,1)S(1)}, u32[]{:S(2)}, u32[]{:S(2)}) collective-permute-start(bf16[256,128]{1,0:T(8,128)(2,1)S(1)} %get-tuple-element.28), channel_id=1, source_target_pairs={{0,28},{4,0},{8,4},{12,8},{16,12},{20,16},{24,20},{28,24},{1,29},{... | collective-permute-start | bytes 196616 | tf_op jit(solution)/shard_map/ppermute | solution.py:274
  23.9 8.0 %collective-permute-start.6 = (bf16[256,128]{1,0:T(8,128)(2,1)S(1)}, bf16[256,128]{1,0:T(8,128)(2,1)S(1)}, u32[]{:S(2)}, u32[]{:S(2)}) collective-permute-start(bf16[256,128]{1,0:T(8,128)(2,1)S(1)} %get-tuple-element.29), channel_id=1, source_target_pairs={{0,24},{4,28},{8,0},{12,4},{16,8},{20,12},{24,16},{28,20},{1,25},{... | collective-permute-start | bytes 196616 | tf_op jit(solution)/shard_map/ppermute | solution.py:274
  23.9 8.0 %collective-permute-start.7 = (bf16[256,128]{1,0:T(8,128)(2,1)S(1)}, bf16[256,128]{1,0:T(8,128)(2,1)S(1)}, u32[]{:S(2)}, u32[]{:S(2)}) collective-permute-start(bf16[256,128]{1,0:T(8,128)(2,1)S(1)} %get-tuple-element.30), channel_id=1, source_target_pairs={{0,20},{4,24},{8,28},{12,0},{16,4},{20,8},{24,12},{28,16},{1,21},{... | collective-permute-start | bytes 196616 | tf_op jit(solution)/shard_map/ppermute | solution.py:274
  24.5 8.9 %collective-permute-start.8 = (bf16[256,128]{1,0:T(8,128)(2,1)S(1)}, bf16[256,128]{1,0:T(8,128)(2,1)S(1)}, u32[]{:S(2)}, u32[]{:S(2)}) collective-permute-start(bf16[256,128]{1,0:T(8,128)(2,1)S(1)} %get-tuple-element.31), channel_id=1, source_target_pairs={{0,16},{4,20},{8,24},{12,28},{16,0},{20,4},{24,8},{28,12},{1,17},{... | collective-permute-start | bytes 196616 | tf_op jit(solution)/shard_map/ppermute | solution.py:274
  27.2 7.6 %collective-permute-start.9 = (bf16[256,128]{1,0:T(8,128)(2,1)S(1)}, bf16[256,128]{1,0:T(8,128)(2,1)S(1)}, u32[]{:S(2)}, u32[]{:S(2)}) collective-permute-start(bf16[256,128]{1,0:T(8,128)(2,1)S(1)} %get-tuple-element.32), channel_id=1, source_target_pairs={{0,12},{4,16},{8,20},{12,24},{16,28},{20,0},{24,4},{28,8},{1,13},{... | collective-permute-start | bytes 196616 | tf_op jit(solution)/shard_map/ppermute | solution.py:274

commit v2 on v1

--- a/solution.py
+++ b/solution.py
@@ -68,10 +68,27 @@
     return jnp.where(allowed, s, -1e30)
 
 
-def early_kernel(shifts, heads, to_exp2, start, lengths_far, q_far, g_far, *refs):
-    pairs = refs[: len(shifts)]
-    q_ref, g_ref, e_ref, gp_ref, stat_ref, lengths, q_sems, g_sems, len_sem = refs[len(shifts) :]
-    block = pairs[0].shape[0] // 2
+def block_terms(pairs, shifts, q, g, low, row, top, to_exp2):
+    block = pairs[0].shape[0] // 2
+    scores = []
+    for n, shift in enumerate(shifts):
+        s = masked_scores(pairs[n], q, low, row, shift)
+        high = jnp.max(s, axis=0, keepdims=True)
+        top = high if top is None else jnp.maximum(top, high)
+        scores.append(s)
+    total, weighted, exps, grads = 0.0, 0.0, [], []
+    for n in range(len(shifts)):
+        e = jnp.exp2((scores[n] - top) * to_exp2)
+        gp = lax.dot_general(pairs[n][block:, :], g, NT, preferred_element_type=F32)
+        total = total + jnp.sum(e, axis=0, keepdims=True)
+        weighted = weighted + jnp.sum(e * gp, axis=0, keepdims=True)
+        exps.append(e)
+        grads.append(gp)
+    return exps, grads, top, total, weighted
+
+
+def own_kernel(heads, to_exp2, start, lengths_far, q_far, g_far, pair_ref, *refs):
+    q_ref, g_ref, e_ref, gp_ref, stat_ref, lengths, q_sems, g_sems, len_sem = refs
     first = start[0]
     tiles = q_ref.shape[0] // TILE
     len_copy = pltpu.make_async_copy(lengths_far, lengths, len_sem)
@@ -92,35 +109,41 @@
         at = pl.ds(index * TILE, TILE)
         row = lax.div(lax.broadcasted_iota(jnp.int32, (1, TILE), 1) + index * TILE, heads)
         low = (doc_begin(first + row, lengths) - first).astype(F32)
-        row = row.astype(F32)
         for c in copies[index]:
             c.wait()
-        q, g = q_ref[at, :], g_ref[at, :]
-        scores, top = [], None
-        for n, shift in enumerate(shifts):
-            s = masked_scores(pairs[n], q, low, row, shift)
-            high = jnp.max(s, axis=0, keepdims=True)
-            top = high if top is None else jnp.maximum(top, high)
-            scores.append(s)
-        total, weighted = 0.0, 0.0
+        exps, grads, top, total, weighted = block_terms(
+            [pair_ref], (0,), q_ref[at, :], g_ref[at, :], low, row.astype(F32), None, to_exp2
+        )
+        e_ref[:, at] = exps[0]
+        gp_ref[:, at] = grads[0]
+        for n, value in enumerate((top, total, weighted, low)):
+            stat_ref[n : n + 1, at] = value
+
+
+def next_kernel(shifts, to_exp2, q_ref, g_ref, stat_ref, *refs):
+    pairs, (e_ref, gp_ref, out_ref) = refs[: len(shifts)], refs[len(shifts) :]
+    block = pairs[0].shape[0] // 2
+    for index in range(q_ref.shape[0] // TILE):
+        at = pl.ds(index * TILE, TILE)
+        old, low = stat_ref[0:1, at], stat_ref[3:4, at]
+        exps, grads, top, total, weighted = block_terms(
+            pairs, shifts, q_ref[at, :], g_ref[at, :], low, None, old, to_exp2
+        )
+        factor = jnp.exp2((old - top) * to_exp2)
         for n in range(len(shifts)):
-            e = jnp.exp2((scores[n] - top) * to_exp2)
-            gp = lax.dot_general(pairs[n][block:, :], g, NT, preferred_element_type=F32)
-            total = total + jnp.sum(e, axis=0, keepdims=True)
-            weighted = weighted + jnp.sum(e * gp, axis=0, keepdims=True)
-            e_ref[n * block : (n + 1) * block, at] = e
-            gp_ref[n * block : (n + 1) * block, at] = gp
-        stat_ref[0:1, at] = top
-        stat_ref[1:2, at] = total
-        stat_ref[2:3, at] = weighted
-        stat_ref[3:4, at] = low
+            e_ref[n * block : (n + 1) * block, at] = exps[n]
+            gp_ref[n * block : (n + 1) * block, at] = grads[n]
+        total = total + stat_ref[1:2, at] * factor
+        weighted = weighted + stat_ref[2:3, at] * factor
+        for n, value in enumerate((top, total, weighted, low, old)):
+            out_ref[n : n + 1, at] = value
 
 
 def main_kernel(early, late, scale, to_exp2, *refs):
-    q_ref, g_ref, e_ref, gp_ref, stat_ref = refs[:5]
-    pairs = refs[5 : 5 + len(late)]
-    p_own, ds_ref = refs[5 + len(late) : 7 + len(late)]
-    sent = refs[7 + len(late) : -2]
+    q_ref, g_ref, e_own, gp_own, e_ref, gp_ref, stat_ref = refs[:7]
+    pairs = refs[7 : 7 + len(late)]
+    p_own, ds_ref = refs[7 + len(late) : 9 + len(late)]
+    sent = refs[9 + len(late) : -2]
     p_ref, acc = refs[-2:]
     back = len(sent)
     block = pairs[0].shape[0] // 2
@@ -135,28 +158,19 @@
 
     def probabilities(index):
         at = pl.ds(index * TILE, TILE)
-        q, g = q_ref[at, :], g_ref[at, :]
-        early_top, low = stat_ref[0:1, at], stat_ref[3:4, at]
-        top, scores = early_top, []
-        for n, shift in enumerate(late):
-            s = masked_scores(pairs[n], q, low, None, shift)
-            top = jnp.maximum(top, jnp.max(s, axis=0, keepdims=True))
-            scores.append(s)
-        factor = jnp.exp2((early_top - top) * to_exp2)
-        total, weighted = stat_ref[1:2, at] * factor, stat_ref[2:3, at] * factor
-        exps, grads = [], []
-        for n in range(len(late)):
-            e = jnp.exp2((scores[n] - top) * to_exp2)
-            gp = lax.dot_general(pairs[n][block:, :], g, NT, preferred_element_type=F32)
-            total = total + jnp.sum(e, axis=0, keepdims=True)
-            weighted = weighted + jnp.sum(e * gp, axis=0, keepdims=True)
-            exps.append(e)
-            grads.append(gp)
-        inverse = 1.0 / total
-        delta = weighted * inverse
+        old, low, own_top = stat_ref[0:1, at], stat_ref[3:4, at], stat_ref[4:5, at]
+        exps, grads, top, total, weighted = block_terms(
+            pairs, late, q_ref[at, :], g_ref[at, :], low, None, old, to_exp2
+        )
+        factor = jnp.exp2((old - top) * to_exp2)
+        inverse = 1.0 / (total + stat_ref[1:2, at] * factor)
+        delta = (weighted + stat_ref[2:3, at] * factor) * inverse
+        p = e_own[:, at] * (jnp.exp2((own_top - top) * to_exp2) * inverse)
+        keep(0, at, p, p * (gp_own[:, at] - delta))
+        factor = factor * inverse
         for n, shift in enumerate(early):
             part = slice(n * block, (n + 1) * block)
-            p = e_ref[part, at] * (factor * inverse)
+            p = e_ref[part, at] * factor
             keep(shift, at, p, p * (gp_ref[part, at] - delta))
         for n, shift in enumerate(late):
             p = exps[n] * inverse
@@ -179,8 +193,9 @@
     sums(tiles - 1)
     for b in range(back):
         at = slice(b * block, (b + 1) * block)
-        sent[b][:block, :] = (acc[0, at, :] * scale).astype(BF16)
-        sent[b][block:, :] = acc[1, at, :].astype(BF16)
+        out = sent[back - 1 - b]
+        out[:block, :] = (acc[0, at, :] * scale).astype(BF16)
+        out[block:, :] = acc[1, at, :].astype(BF16)
 
 
 def rest_kernel(back, scale, *refs):
@@ -287,36 +302,38 @@
         )(lengths, start, q, g, pair, *others)
         returned = [turn(sent[b - 1], -b) for b in range(1, back + 1)]
     else:
-        early = (0,) + tuple(range(back, back - EARLY, -1))
+        early = tuple(range(back, back - EARLY, -1))
         late = tuple(range(1, back + 1 - EARLY))
-        tall = len(early) * rows
         tiles = flat // TILE
-        q, g, e, gp, stat = call(
-            functools.partial(early_kernel, early, heads, to_exp2),
-            [
-                shape(flat, width),
-                shape(flat, width),
-                shape(tall, flat, dtype=F32),
-                shape(tall, flat, dtype=F32),
-                shape(8, flat, dtype=F32),
-            ],
+
+        def wide(n):
+            return shape(n * rows, flat, dtype=F32)
+
+        q, g, e_own, gp_own, stat = call(
+            functools.partial(own_kernel, heads, to_exp2),
+            [shape(flat, width), shape(flat, width), wide(1), wide(1), shape(8, flat, dtype=F32)],
             [
                 pltpu.SMEM(lengths.shape, jnp.int32),
                 pltpu.SemaphoreType.DMA((tiles,)),
                 pltpu.SemaphoreType.DMA((tiles,)),
                 pltpu.SemaphoreType.DMA,
             ],
-            flops=2**29,
+            flops=2**28,
             far=(1, 2, 3),
-        )(start, lengths, q, g, *([pair, *others][shift] for shift in early))
+        )(start, lengths, q, g, pair)
+        e, gp, stat = call(
+            functools.partial(next_kernel, early, to_exp2),
+            [wide(EARLY), wide(EARLY), shape(8, flat, dtype=F32)],
+            flops=2**28,
+        )(q, g, stat, *(others[shift - 1] for shift in early))
         p_own, ds, *sent = call(
             functools.partial(main_kernel, early, late, scale, to_exp2),
             [shape(rows, flat), shape((back + 1) * rows, flat)] + [partial] * back,
             [pltpu.VMEM((back * rows, flat), BF16), pltpu.VMEM((2, back * rows, width), F32)],
             mib=16,
             flops=2**31,
-        )(q, g, e, gp, stat, *(others[shift - 1] for shift in late))
-        returned = [turn(sent[b - 1], -b) for b in range(1, back + 1)]
+        )(q, g, e_own, gp_own, e, gp, stat, *(others[shift - 1] for shift in late))
+        returned = [turn(sent[back - b], -b) for b in range(back, 0, -1)]
         dq, own = call(
             functools.partial(rest_kernel, back, scale),
             [shape(flat, width), shape(2 * rows, width, dtype=F32)],

time: 35.7 us -> 32.9 us (0.922)
  waiting for transfers between devices: 4.03 us -> 2.04 us
  starting transfers between devices: 20.5 us -> 19.5 us
    ppermute x10, waiting for transfers between devices: 4.03 us -> 2.04 us  [turn(): return lax.ppermute(x, 'ctx', [(i, (i + by) % count) for i in range(count)])]
    ppermute x10, starting transfers between devices: 20.5 us -> 19.5 us  [turn(): return lax.ppermute(x, 'ctx', [(i, (i + by) % count) for i in range(count)])]
    pallas_call x5 -> x6, Pallas kernels: 10.3 us -> 10.5 us  [run(): pl.pallas_call(kernel, out_shape=outs, in_specs=in_specs, out_specs=[VMEM...]
  transfers between devices with their start and end apart: 10 -> 10, of which waited for: 3 -> 2; matrix products, arithmetic and copies ran while one was open for 0% -> 0% of each run, Pallas kernels for 16% -> 18%
where the time goes in v2:
time: 32.9 us; the launch traced here: 32.6 us
  starting transfers between devices  19.5 us (59%)
  Pallas kernels  10.5 us (32%)
  waiting for transfers between devices  2.04 us (6%)
  between operations  0.69 us (2%)
    ppermute x10, starting transfers between devices, turn(): return lax.ppermute(x, 'ctx', [(i, (i + by) % count) for i in range(count)])  19.5 us
    pallas_call x6, Pallas kernels, run(): pl.pallas_call(kernel, out_shape=outs, in_specs=in_specs, out_specs=[VMEM...  10.5 us
    ppermute x10, waiting for transfers between devices, turn(): return lax.ppermute(x, 'ctx', [(i, (i + by) % count) for i in range(count)])  2.04 us
  transfers between devices with their start and end apart: 10, of which 2 were waited for; matrix products, arithmetic and copies ran while one was open for 0% of the time, Pallas kernels for 18%

profile of v2, /device:TPU:0, one launch (start us, length us, event | category | flops | bytes accessed | tf_op | source)
XLA Modules:
  0.0 32.6 jit_solution(12201922134727759344)
XLA Ops:
  0.6 0.8 %shard_map.76.pair_ref.refs_4_ = bf16[256,128]{1,0:T(8,128)(2,1)S(1)} custom-call(bf16[128,128]{1,0:T(8,128)(2,1)} %k_far.1, bf16[128,128]{1,0:T(8,128)(2,1)} %v_far.1), custom_call_target="tpu_custom_call" | custom-call | bytes 1048576 | tf_op jit(solution)/shard_map/pallas_call | solution.py:28
  1.4 4.1 %collective-permute-start.1 = (bf16[256,128]{1,0:T(8,128)(2,1)S(1)}, bf16[256,128]{1,0:T(8,128)(2,1)S(1)}, u32[]{:S(2)}, u32[]{:S(2)}) collective-permute-start(bf16[256,128]{1,0:T(8,128)(2,1)S(1)} %shard_map.76.pair_ref.refs_4_), channel_id=1, source_target_pairs={{0,16},{4,20},{8,24},{12,28},{16,0},{20,4},{24,8},{28,12},{1,17},{... | collective-permute-start | bytes 196616 | tf_op jit(solution)/shard_map/ppermute | solution.py:289
  5.5 1.3 %collective-permute-start = (bf16[256,128]{1,0:T(8,128)(2,1)S(1)}, bf16[256,128]{1,0:T(8,128)(2,1)S(1)}, u32[]{:S(2)}, u32[]{:S(2)}) collective-permute-start(bf16[256,128]{1,0:T(8,128)(2,1)S(1)} %shard_map.76.pair_ref.refs_4_), channel_id=1, source_target_pairs={{0,20},{4,24},{8,28},{12,0},{16,4},{20,8},{24,12},{28,16},{1,21},{... | collective-permute-start | bytes 196616 | tf_op jit(solution)/shard_map/ppermute | solution.py:289
  6.8 1.7 %collective-permute-start.4 = (bf16[256,128]{1,0:T(8,128)(2,1)S(1)}, bf16[256,128]{1,0:T(8,128)(2,1)S(1)}, u32[]{:S(2)}, u32[]{:S(2)}) collective-permute-start(bf16[256,128]{1,0:T(8,128)(2,1)S(1)} %shard_map.76.pair_ref.refs_4_), channel_id=1, source_target_pairs={{0,12},{4,16},{8,20},{12,24},{16,28},{20,0},{24,4},{28,8},{1,13},{... | collective-permute-start | bytes 196616 | tf_op jit(solution)/shard_map/ppermute | solution.py:289
  8.5 1.6 %collective-permute-start.3 = (bf16[256,128]{1,0:T(8,128)(2,1)S(1)}, bf16[256,128]{1,0:T(8,128)(2,1)S(1)}, u32[]{:S(2)}, u32[]{:S(2)}) collective-permute-start(bf16[256,128]{1,0:T(8,128)(2,1)S(1)} %shard_map.76.pair_ref.refs_4_), channel_id=1, source_target_pairs={{0,8},{4,12},{8,16},{12,20},{16,24},{20,28},{24,0},{28,4},{1,9},{5... | collective-permute-start | bytes 196616 | tf_op jit(solution)/shard_map/ppermute | solution.py:289
  10.0 2.4 %collective-permute-start.2 = (bf16[256,128]{1,0:T(8,128)(2,1)S(1)}, bf16[256,128]{1,0:T(8,128)(2,1)S(1)}, u32[]{:S(2)}, u32[]{:S(2)}) collective-permute-start(bf16[256,128]{1,0:T(8,128)(2,1)S(1)} %shard_map.76.pair_ref.refs_4_), channel_id=1, source_target_pairs={{0,4},{4,8},{8,12},{12,16},{16,20},{20,24},{24,28},{28,0},{1,5},{5... | collective-permute-start | bytes 196616 | tf_op jit(solution)/shard_map/ppermute | solution.py:289
  12.4 3.0 %shard_map.77 = (bf16[2048,128]{1,0:T(8,128)(2,1)S(1)}, bf16[2048,128]{1,0:T(8,128)(2,1)S(1)}, f32[128,2048]{1,0:T(8,128)S(1)}, f32[128,2048]{1,0:T(8,128)S(1)}, f32[8,2048]{1,0:T(8,128)S(1)}) custom-call(s32[1]{0:T(128)} %bitcast.start, s32[16]{0:T(128)} %lengths_far.1, bf16[2048,128]{1,0:T(8,128)(2,1)} %bitcast.4, bf16[2048,128]{1,0:T(8,128)(2,1)} %bitcast.5, ...), custom_call_target="tpu_custom_call" | custom-call | flops 268435456 | bytes 1048576 | tf_op jit(solution)/shard_map/pallas_call | solution.py:28
  15.4 0.0 collective-permute-done.1.refs_1_.refs_8_
  15.4 0.0 collective-permute-done.refs_0_.refs_9_
  15.4 1.1 %shard_map.78 = (f32[256,2048]{1,0:T(8,128)S(1)}, f32[256,2048]{1,0:T(8,128)S(1)}, f32[8,2048]{1,0:T(8,128)S(1)}) custom-call(bf16[2048,128]{1,0:T(8,128)(2,1)S(1)} %get-tuple-element.22.q_ref.refs_0_, bf16[2048,128]{1,0:T(8,128)(2,1)S(1)} %get-tuple-element.23.g_ref.refs_1_, f32[8,2048]{1,0:T(8,128)S(1)} %get-tuple-element.26.stat_ref, ...), custom_call_target="tpu_custom_call" | custom-call | flops 268435456 | bytes 1048576 | tf_op jit(solution)/shard_map/pallas_call | solution.py:28
  16.5 0.8 %collective-permute-done.4.refs_9_.refs_7_ = bf16[256,128]{1,0:T(8,128)(2,1)S(1)} collective-permute-done((bf16[256,128]{1,0:T(8,128)(2,1)S(1)}, bf16[256,128]{1,0:T(8,128)(2,1)S(1)}, u32[]{:S(2)}, u32[]{:S(2)}) %collective-permute-start.4) | collective-permute-done | bytes 65568 | tf_op jit(solution)/shard_map/ppermute | solution.py:289
  17.3 0.0 collective-permute-done.3.refs_8_.refs_6_
  17.3 0.0 collective-permute-done.2.refs_7_.refs_5_
  17.3 3.3 %shard_map.79 = (bf16[128,2048]{1,0:T(8,128)(2,1)S(1)}, bf16[768,2048]{1,0:T(8,128)(2,1)S(1)}, bf16[256,128]{1,0:T(8,128)(2,1)S(1)}, bf16[256,128]{1,0:T(8,128)(...) custom-call(bf16[2048,128]{1,0:T(8,128)(2,1)S(1)} %get-tuple-element.22.q_ref.ref, ...), custom_call_target="tpu_custom_call" | custom-call | flops 2147483648 | bytes 1048576 | tf_op jit(solution)/shard_map/pallas_call | solution.py:28
  20.6 0.4 %collective-permute-start.5 = (bf16[256,128]{1,0:T(8,128)(2,1)S(1)}, bf16[256,128]{1,0:T(8,128)(2,1)S(1)}, u32[]{:S(2)}, u32[]{:S(2)}) collective-permute-start(bf16[256,128]{1,0:T(8,128)(2,1)S(1)} %get-tuple-element.34), channel_id=1, source_target_pairs={{0,12},{4,16},{8,20},{12,24},{16,28},{20,0},{24,4},{28,8},{1,13},{... | collective-permute-start | bytes 196616 | tf_op jit(solution)/shard_map/ppermute | solution.py:289
  21.1 2.0 %collective-permute-start.6 = (bf16[256,128]{1,0:T(8,128)(2,1)S(1)}, bf16[256,128]{1,0:T(8,128)(2,1)S(1)}, u32[]{:S(2)}, u32[]{:S(2)}) collective-permute-start(bf16[256,128]{1,0:T(8,128)(2,1)S(1)} %get-tuple-element.35), channel_id=1, source_target_pairs={{0,16},{4,20},{8,24},{12,28},{16,0},{20,4},{24,8},{28,12},{1,17},{... | collective-permute-start | bytes 196616 | tf_op jit(solution)/shard_map/ppermute | solution.py:289
  23.0 3.7 %collective-permute-start.7 = (bf16[256,128]{1,0:T(8,128)(2,1)S(1)}, bf16[256,128]{1,0:T(8,128)(2,1)S(1)}, u32[]{:S(2)}, u32[]{:S(2)}) collective-permute-start(bf16[256,128]{1,0:T(8,128)(2,1)S(1)} %get-tuple-element.36), channel_id=1, source_target_pairs={{0,20},{4,24},{8,28},{12,0},{16,4},{20,8},{24,12},{28,16},{1,21},{... | collective-permute-start | bytes 196616 | tf_op jit(solution)/shard_map/ppermute | solution.py:289
  26.8 0.0 collective-permute-start.8
  26.8 2.3 %collective-permute-start.9 = (bf16[256,128]{1,0:T(8,128)(2,1)S(1)}, bf16[256,128]{1,0:T(8,128)(2,1)S(1)}, u32[]{:S(2)}, u32[]{:S(2)}) collective-permute-start(bf16[256,128]{1,0:T(8,128)(2,1)S(1)} %get-tuple-element.38), channel_id=1, source_target_pairs={{0,28},{4,0},{8,4},{12,8},{16,12},{20,16},{24,20},{28,24},{1,29},{... | collective-permute-start | bytes 196616 | tf_op jit(solution)/shard_map/ppermute | solution.py:289
  29.1 1.7 %shard_map.80 = (bf16[2048,128]{1,0:T(8,128)(2,1)}, f32[256,128]{1,0:T(8,128)S(1)}) custom-call(bf16[2048,128]{1,0:T(8,128)(2,1)S(1)} %get-tuple-element.22.q_ref.refs_0_, bf16[2048,128]{1,0:T(8,128)(2,1)S(1)} %get-tuple-element.23.g_ref.refs_1_, bf16[128,2048]{1,0:T(8,128)(2,1)S(1)} %get-tuple-element.30.refs_2_, ...), custom_call_target="tpu_custom_call" | custom-call | flops 536870912 | bytes 1048576 | tf_op jit(solution)/shard_map/pallas_call | solution.py:28
  30.8 0.0 collective-permute-done.5.refs_0_
  30.8 0.0 collective-permute-done.6.refs_1_
  30.8 0.0 collective-permute-done.7.refs_2_
  30.8 1.2 %collective-permute-done.8.refs_3_ = bf16[256,128]{1,0:T(8,128)(2,1)S(1)} collective-permute-done((bf16[256,128]{1,0:T(8,128)(2,1)S(1)}, bf16[256,128]{1,0:T(8,128)(2,1)S(1)}, u32[]{:S(2)}, u32[]{:S(2)}) %collective-permute-start.8) | collective-permute-done | bytes 65568 | tf_op jit(solution)/shard_map/ppermute | solution.py:289
  32.0 0.0 collective-permute-done.9.refs_4_
  32.0 0.7 %shard_map.81 = (bf16[128,128]{1,0:T(8,128)(2,1)}, bf16[128,128]{1,0:T(8,128)(2,1)}) custom-call(f32[256,128]{1,0:T(8,128)S(1)} %get-tuple-element.33.own, bf16[256,128]{1,0:T(8,128)(2,1)S(1)} %collective-permute-done.5.refs_0_, bf16[256,128]{1,0:T(8,128)(2,1)S(1)} %collective-permute-done.6.refs_1_, bf16[256,128]{1,0:T(8,128)(2,1)S(1)} %collective-permute-done.7.refs_2_, ...), custom_call_target="tpu_custom_call" | custom-call | bytes 1048576 | tf_op jit(solution)/shard_map/pallas_call | solution.py:28
Async XLA Ops:
  1.4 14.0 %collective-permute-start.1 = (bf16[256,128]{1,0:T(8,128)(2,1)S(1)}, bf16[256,128]{1,0:T(8,128)(2,1)S(1)}, u32[]{:S(2)}, u32[]{:S(2)}) collective-permute-start(bf16[256,128]{1,0:T(8,128)(2,1)S(1)} %shard_map.76.pair_ref.refs_4_), channel_id=1, source_target_pairs={{0,16},{4,20},{8,24},{12,28},{16,0},{20,4},{24,8},{28,12},{1,17},{... | collective-permute-start | bytes 196616 | tf_op jit(solution)/shard_map/ppermute | solution.py:289
  5.5 9.9 %collective-permute-start = (bf16[256,128]{1,0:T(8,128)(2,1)S(1)}, bf16[256,128]{1,0:T(8,128)(2,1)S(1)}, u32[]{:S(2)}, u32[]{:S(2)}) collective-permute-start(bf16[256,128]{1,0:T(8,128)(2,1)S(1)} %shard_map.76.pair_ref.refs_4_), channel_id=1, source_target_pairs={{0,20},{4,24},{8,28},{12,0},{16,4},{20,8},{24,12},{28,16},{1,21},{... | collective-permute-start | bytes 196616 | tf_op jit(solution)/shard_map/ppermute | solution.py:289
  6.8 10.5 %collective-permute-start.4 = (bf16[256,128]{1,0:T(8,128)(2,1)S(1)}, bf16[256,128]{1,0:T(8,128)(2,1)S(1)}, u32[]{:S(2)}, u32[]{:S(2)}) collective-permute-start(bf16[256,128]{1,0:T(8,128)(2,1)S(1)} %shard_map.76.pair_ref.refs_4_), channel_id=1, source_target_pairs={{0,12},{4,16},{8,20},{12,24},{16,28},{20,0},{24,4},{28,8},{1,13},{... | collective-permute-start | bytes 196616 | tf_op jit(solution)/shard_map/ppermute | solution.py:289
  8.5 8.9 %collective-permute-start.3 = (bf16[256,128]{1,0:T(8,128)(2,1)S(1)}, bf16[256,128]{1,0:T(8,128)(2,1)S(1)}, u32[]{:S(2)}, u32[]{:S(2)}) collective-permute-start(bf16[256,128]{1,0:T(8,128)(2,1)S(1)} %shard_map.76.pair_ref.refs_4_), channel_id=1, source_target_pairs={{0,8},{4,12},{8,16},{12,20},{16,24},{20,28},{24,0},{28,4},{1,9},{5... | collective-permute-start | bytes 196616 | tf_op jit(solution)/shard_map/ppermute | solution.py:289
  10.0 7.3 %collective-permute-start.2 = (bf16[256,128]{1,0:T(8,128)(2,1)S(1)}, bf16[256,128]{1,0:T(8,128)(2,1)S(1)}, u32[]{:S(2)}, u32[]{:S(2)}) collective-permute-start(bf16[256,128]{1,0:T(8,128)(2,1)S(1)} %shard_map.76.pair_ref.refs_4_), channel_id=1, source_target_pairs={{0,4},{4,8},{8,12},{12,16},{16,20},{20,24},{24,28},{28,0},{1,5},{5... | collective-permute-start | bytes 196616 | tf_op jit(solution)/shard_map/ppermute | solution.py:289
  20.6 10.2 %collective-permute-start.5 = (bf16[256,128]{1,0:T(8,128)(2,1)S(1)}, bf16[256,128]{1,0:T(8,128)(2,1)S(1)}, u32[]{:S(2)}, u32[]{:S(2)}) collective-permute-start(bf16[256,128]{1,0:T(8,128)(2,1)S(1)} %get-tuple-element.34), channel_id=1, source_target_pairs={{0,12},{4,16},{8,20},{12,24},{16,28},{20,0},{24,4},{28,8},{1,13},{... | collective-permute-start | bytes 196616 | tf_op jit(solution)/shard_map/ppermute | solution.py:289
  21.1 9.7 %collective-permute-start.6 = (bf16[256,128]{1,0:T(8,128)(2,1)S(1)}, bf16[256,128]{1,0:T(8,128)(2,1)S(1)}, u32[]{:S(2)}, u32[]{:S(2)}) collective-permute-start(bf16[256,128]{1,0:T(8,128)(2,1)S(1)} %get-tuple-element.35), channel_id=1, source_target_pairs={{0,16},{4,20},{8,24},{12,28},{16,0},{20,4},{24,8},{28,12},{1,17},{... | collective-permute-start | bytes 196616 | tf_op jit(solution)/shard_map/ppermute | solution.py:289
  23.0 7.8 %collective-permute-start.7 = (bf16[256,128]{1,0:T(8,128)(2,1)S(1)}, bf16[256,128]{1,0:T(8,128)(2,1)S(1)}, u32[]{:S(2)}, u32[]{:S(2)}) collective-permute-start(bf16[256,128]{1,0:T(8,128)(2,1)S(1)} %get-tuple-element.36), channel_id=1, source_target_pairs={{0,20},{4,24},{8,28},{12,0},{16,4},{20,8},{24,12},{28,16},{1,21},{... | collective-permute-start | bytes 196616 | tf_op jit(solution)/shard_map/ppermute | solution.py:289
  26.8 5.2 %collective-permute-start.8 = (bf16[256,128]{1,0:T(8,128)(2,1)S(1)}, bf16[256,128]{1,0:T(8,128)(2,1)S(1)}, u32[]{:S(2)}, u32[]{:S(2)}) collective-permute-start(bf16[256,128]{1,0:T(8,128)(2,1)S(1)} %get-tuple-element.37), channel_id=1, source_target_pairs={{0,24},{4,28},{8,0},{12,4},{16,8},{20,12},{24,16},{28,20},{1,25},{... | collective-permute-start | bytes 196616 | tf_op jit(solution)/shard_map/ppermute | solution.py:289
  26.8 5.2 %collective-permute-start.9 = (bf16[256,128]{1,0:T(8,128)(2,1)S(1)}, bf16[256,128]{1,0:T(8,128)(2,1)S(1)}, u32[]{:S(2)}, u32[]{:S(2)}) collective-permute-start(bf16[256,128]{1,0:T(8,128)(2,1)S(1)} %get-tuple-element.38), channel_id=1, source_target_pairs={{0,28},{4,0},{8,4},{12,8},{16,12},{20,16},{24,20},{28,24},{1,29},{... | collective-permute-start | bytes 196616 | tf_op jit(solution)/shard_map/ppermute | solution.py:289

commit v3 on v2

--- a/solution.py
+++ b/solution.py
@@ -10,7 +10,7 @@
 
 NT = (((1,), (1,)), ((), ()))
 TILE = 256
-EARLY = 2
+GROUPS = ((0, 1), (2, 3))
 F32, BF16 = jnp.float32, jnp.bfloat16
 VMEM = pl.BlockSpec(memory_space=pltpu.VMEM)
 SMEM = pl.BlockSpec(memory_space=pltpu.SMEM)
@@ -58,28 +58,23 @@
         c.wait()
 
 
-def masked_scores(pair_ref, q, low, row, shift):
-    block = pair_ref.shape[0] // 2
+def block_terms(pairs, bounds, q, g, row, top, to_exp2):
+    block = pairs[0].shape[0] // 2
     key = lax.broadcasted_iota(jnp.int32, (block, q.shape[0]), 0).astype(F32)
-    s = lax.dot_general(pair_ref[:block, :], q, NT, preferred_element_type=F32)
-    allowed = key >= low + float(shift * block)
-    if shift == 0:
-        allowed = allowed & (key <= row)
-    return jnp.where(allowed, s, -1e30)
-
-
-def block_terms(pairs, shifts, q, g, low, row, top, to_exp2):
-    block = pairs[0].shape[0] // 2
     scores = []
-    for n, shift in enumerate(shifts):
-        s = masked_scores(pairs[n], q, low, row, shift)
+    for pair, bound in zip(pairs, bounds):
+        s = lax.dot_general(pair[:block, :], q, NT, preferred_element_type=F32)
+        allowed = key >= bound
+        if row is not None:
+            allowed = allowed & (key <= row)
+        s = jnp.where(allowed, s, -1e30)
         high = jnp.max(s, axis=0, keepdims=True)
         top = high if top is None else jnp.maximum(top, high)
         scores.append(s)
     total, weighted, exps, grads = 0.0, 0.0, [], []
-    for n in range(len(shifts)):
-        e = jnp.exp2((scores[n] - top) * to_exp2)
-        gp = lax.dot_general(pairs[n][block:, :], g, NT, preferred_element_type=F32)
+    for pair, s in zip(pairs, scores):
+        e = jnp.exp2((s - top) * to_exp2)
+        gp = lax.dot_general(pair[block:, :], g, NT, preferred_element_type=F32)
         total = total + jnp.sum(e, axis=0, keepdims=True)
         weighted = weighted + jnp.sum(e * gp, axis=0, keepdims=True)
         exps.append(e)
@@ -87,9 +82,16 @@
     return exps, grads, top, total, weighted
 
 
-def own_kernel(heads, to_exp2, start, lengths_far, q_far, g_far, pair_ref, *refs):
-    q_ref, g_ref, e_ref, gp_ref, stat_ref, lengths, q_sems, g_sems, len_sem = refs
+def own_kernel(heads, shifts, to_exp2, start, lengths_far, q_far, g_far, pair_ref, *refs):
+    q_ref, g_ref, e_ref, gp_ref, stat_ref, bound_ref, lengths, q_sems, g_sems, len_sem = refs
     first = start[0]
+    block = pair_ref.shape[0] // 2
+    offsets = []
+    for shift in shifts:
+        offset = jnp.int32(0)
+        for c, s in enumerate(shift):
+            offset = jnp.where(first == c * block, s * block, offset)
+        offsets.append(offset)
     tiles = q_ref.shape[0] // TILE
     len_copy = pltpu.make_async_copy(lengths_far, lengths, len_sem)
     len_copy.start()
@@ -108,73 +110,78 @@
     for index in range(tiles):
         at = pl.ds(index * TILE, TILE)
         row = lax.div(lax.broadcasted_iota(jnp.int32, (1, TILE), 1) + index * TILE, heads)
-        low = (doc_begin(first + row, lengths) - first).astype(F32)
+        low = doc_begin(first + row, lengths) - first
+        for k, offset in enumerate(offsets):
+            bound_ref[k : k + 1, at] = (low + offset).astype(F32)
         for c in copies[index]:
             c.wait()
         exps, grads, top, total, weighted = block_terms(
-            [pair_ref], (0,), q_ref[at, :], g_ref[at, :], low, row.astype(F32), None, to_exp2
+            [pair_ref], [low.astype(F32)], q_ref[at, :], g_ref[at, :], row.astype(F32), None, to_exp2
         )
         e_ref[:, at] = exps[0]
         gp_ref[:, at] = grads[0]
-        for n, value in enumerate((top, total, weighted, low)):
+        for n, value in enumerate((total, weighted, top)):
             stat_ref[n : n + 1, at] = value
 
 
-def next_kernel(shifts, to_exp2, q_ref, g_ref, stat_ref, *refs):
-    pairs, (e_ref, gp_ref, out_ref) = refs[: len(shifts)], refs[len(shifts) :]
+def next_kernel(group, depth, to_exp2, q_ref, g_ref, bound_ref, stat_ref, *refs):
+    pairs, (e_ref, gp_ref, out_ref) = refs[: len(group)], refs[len(group) :]
     block = pairs[0].shape[0] // 2
     for index in range(q_ref.shape[0] // TILE):
         at = pl.ds(index * TILE, TILE)
-        old, low = stat_ref[0:1, at], stat_ref[3:4, at]
+        old = stat_ref[1 + depth : 2 + depth, at]
         exps, grads, top, total, weighted = block_terms(
-            pairs, shifts, q_ref[at, :], g_ref[at, :], low, None, old, to_exp2
+            pairs, [bound_ref[k : k + 1, at] for k in group], q_ref[at, :], g_ref[at, :], None, old, to_exp2
         )
         factor = jnp.exp2((old - top) * to_exp2)
-        for n in range(len(shifts)):
+        for n in range(len(group)):
             e_ref[n * block : (n + 1) * block, at] = exps[n]
             gp_ref[n * block : (n + 1) * block, at] = grads[n]
-        total = total + stat_ref[1:2, at] * factor
-        weighted = weighted + stat_ref[2:3, at] * factor
-        for n, value in enumerate((top, total, weighted, low, old)):
-            out_ref[n : n + 1, at] = value
-
-
-def main_kernel(early, late, scale, to_exp2, *refs):
-    q_ref, g_ref, e_own, gp_own, e_ref, gp_ref, stat_ref = refs[:7]
-    pairs = refs[7 : 7 + len(late)]
-    p_own, ds_ref = refs[7 + len(late) : 9 + len(late)]
-    sent = refs[9 + len(late) : -2]
+        out_ref[0:1, at] = total + stat_ref[0:1, at] * factor
+        out_ref[1:2, at] = weighted + stat_ref[1:2, at] * factor
+        out_ref[2 : 2 + depth, at] = stat_ref[2 : 2 + depth, at]
+        out_ref[2 + depth : 3 + depth, at] = top
+
+
+def main_kernel(groups, late, scale, to_exp2, *refs):
+    q_ref, g_ref, bound_ref, stat_ref = refs[:4]
+    depth = len(groups)
+    made = [refs[4 + 2 * n : 6 + 2 * n] for n in range(depth)]
+    refs = refs[4 + 2 * depth :]
+    pairs = refs[: len(late)]
+    p_own, ds_ref = refs[len(late) : 2 + len(late)]
+    sent = refs[2 + len(late) : -2]
     p_ref, acc = refs[-2:]
     back = len(sent)
     block = pairs[0].shape[0] // 2
     tiles = q_ref.shape[0] // TILE
 
-    def keep(shift, at, p, ds):
-        if shift == 0:
+    def keep(k, at, p, ds):
+        if k < 0:
             p_own[:, at] = p.astype(BF16)
         else:
-            p_ref[(shift - 1) * block : shift * block, at] = p.astype(BF16)
-        ds_ref[shift * block : (shift + 1) * block, at] = ds.astype(BF16)
+            p_ref[k * block : (k + 1) * block, at] = p.astype(BF16)
+        ds_ref[(k + 1) * block : (k + 2) * block, at] = ds.astype(BF16)
 
     def probabilities(index):
         at = pl.ds(index * TILE, TILE)
-        old, low, own_top = stat_ref[0:1, at], stat_ref[3:4, at], stat_ref[4:5, at]
+        old = stat_ref[1 + depth : 2 + depth, at]
         exps, grads, top, total, weighted = block_terms(
-            pairs, late, q_ref[at, :], g_ref[at, :], low, None, old, to_exp2
+            pairs, [bound_ref[k : k + 1, at] for k in late], q_ref[at, :], g_ref[at, :], None, old, to_exp2
         )
         factor = jnp.exp2((old - top) * to_exp2)
-        inverse = 1.0 / (total + stat_ref[1:2, at] * factor)
-        delta = (weighted + stat_ref[2:3, at] * factor) * inverse
-        p = e_own[:, at] * (jnp.exp2((own_top - top) * to_exp2) * inverse)
-        keep(0, at, p, p * (gp_own[:, at] - delta))
-        factor = factor * inverse
-        for n, shift in enumerate(early):
-            part = slice(n * block, (n + 1) * block)
-            p = e_ref[part, at] * factor
-            keep(shift, at, p, p * (gp_ref[part, at] - delta))
-        for n, shift in enumerate(late):
+        inverse = 1.0 / (total + stat_ref[0:1, at] * factor)
+        delta = (weighted + stat_ref[1:2, at] * factor) * inverse
+        for d, group in enumerate(groups):
+            e_ref, gp_ref = made[d]
+            factor = jnp.exp2((stat_ref[2 + d : 3 + d, at] - top) * to_exp2) * inverse
+            for n, k in enumerate(group):
+                part = slice(n * block, (n + 1) * block)
+                p = e_ref[part, at] * factor
+                keep(k, at, p, p * (gp_ref[part, at] - delta))
+        for n, k in enumerate(late):
             p = exps[n] * inverse
-            keep(shift, at, p, p * (grads[n] - delta))
+            keep(k, at, p, p * (grads[n] - delta))
 
     def sums(index):
         at = pl.ds(index * TILE, TILE)
@@ -193,7 +200,7 @@
     sums(tiles - 1)
     for b in range(back):
         at = slice(b * block, (b + 1) * block)
-        out = sent[back - 1 - b]
+        out = sent[b]
         out[:block, :] = (acc[0, at, :] * scale).astype(BF16)
         out[block:, :] = acc[1, at, :].astype(BF16)
 
@@ -285,33 +292,43 @@
     q, g = queries.reshape(-1, width), grad_out.reshape(-1, width)
     flat = rows * heads
 
-    def turn(x, by):
-        return lax.ppermute(x, "ctx", [(i, (i + by) % count) for i in range(count)])
+    perms = [[(c + b) % count for c in range(count)] for b in range(back, 0, -1)]
+    forth = [list(enumerate(p)) for p in perms]
+    here = [[(d, c) for c, d in pairs] for pairs in forth]
+    shifts = [[c - dict(pairs)[c] for c in range(count)] for pairs in here]
+    shifts = [[s if 0 < s <= back else 2 * count for s in row] for row in shifts]
+
+    def fetch(x, k):
+        return lax.ppermute(x, "ctx", forth[k])
+
+    def give_back(x, k):
+        return lax.ppermute(x, "ctx", here[k])
 
     pair = call(pack_kernel, [shape(2 * rows, width)], [pltpu.SemaphoreType.DMA((2,))], mib=1, far=(0, 1))(
         keys, values
     )[0]
-    others = [turn(pair, b) for b in range(1, back + 1)]
+    others = [fetch(pair, k) for k in range(back)]
     partial = shape(2 * rows, width)
     if back > 7:
+        others = others[::-1]
         dq, own, *sent = call(
             functools.partial(whole_kernel, back, heads, scale, to_exp2),
             [shape(flat, width), shape(2 * rows, width, dtype=F32)] + [partial] * back,
             [pltpu.VMEM((back + 1, 2 * rows, width), F32)],
             mib=48,
         )(lengths, start, q, g, pair, *others)
-        returned = [turn(sent[b - 1], -b) for b in range(1, back + 1)]
+        returned = [give_back(sent[back - 1 - k], k) for k in range(back)]
     else:
-        early = tuple(range(back, back - EARLY, -1))
-        late = tuple(range(1, back + 1 - EARLY))
+        groups = [(-1,), *GROUPS] if back == 5 else [(-1,)]
+        late = [k for k in range(back) if k not in sum(groups, ())]
         tiles = flat // TILE
 
         def wide(n):
             return shape(n * rows, flat, dtype=F32)
 
-        q, g, e_own, gp_own, stat = call(
-            functools.partial(own_kernel, heads, to_exp2),
-            [shape(flat, width), shape(flat, width), wide(1), wide(1), shape(8, flat, dtype=F32)],
+        q, g, e, gp, stat, bound = call(
+            functools.partial(own_kernel, heads, shifts, to_exp2),
+            [shape(flat, width)] * 2 + [wide(1)] * 2 + [shape(8, flat, dtype=F32)] * 2,
             [
                 pltpu.SMEM(lengths.shape, jnp.int32),
                 pltpu.SemaphoreType.DMA((tiles,)),
@@ -321,19 +338,22 @@
             flops=2**28,
             far=(1, 2, 3),
         )(start, lengths, q, g, pair)
-        e, gp, stat = call(
-            functools.partial(next_kernel, early, to_exp2),
-            [wide(EARLY), wide(EARLY), shape(8, flat, dtype=F32)],
-            flops=2**28,
-        )(q, g, stat, *(others[shift - 1] for shift in early))
+        made = [e, gp]
+        for depth, group in enumerate(groups[1:], 1):
+            e, gp, stat = call(
+                functools.partial(next_kernel, group, depth, to_exp2),
+                [wide(len(group))] * 2 + [shape(8, flat, dtype=F32)],
+                flops=2**28,
+            )(q, g, bound, stat, *(others[k] for k in group))
+            made += [e, gp]
         p_own, ds, *sent = call(
-            functools.partial(main_kernel, early, late, scale, to_exp2),
+            functools.partial(main_kernel, groups, late, scale, to_exp2),
             [shape(rows, flat), shape((back + 1) * rows, flat)] + [partial] * back,
             [pltpu.VMEM((back * rows, flat), BF16), pltpu.VMEM((2, back * rows, width), F32)],
             mib=16,
             flops=2**31,
-        )(q, g, e_own, gp_own, e, gp, stat, *(others[shift - 1] for shift in late))
-        returned = [turn(sent[back - b], -b) for b in range(back, 0, -1)]
+        )(q, g, bound, stat, *made, *(others[k] for k in late))
+        returned = [give_back(sent[k], k) for k in range(back)]
         dq, own = call(
             functools.partial(rest_kernel, back, scale),
             [shape(flat, width), shape(2 * rows, width, dtype=F32)],

time: 32.9 us -> 32 us (0.973)
  waiting for transfers between devices: 2.04 us -> 1.04 us
    ppermute x10, waiting for transfers between devices: 2.04 us -> 1.04 us  [the longest x5 0.85 us: fetch(): return lax.ppermute(x, 'ctx', forth[k])]
    pallas_call x6 -> x7, Pallas kernels: 10.5 us -> 10.6 us  [run(): pl.pallas_call(kernel, out_shape=outs, in_specs=in_specs, out_specs=[VMEM...]
  transfers between devices with their start and end apart: 10 -> 10, of which waited for: 2 -> 2; matrix products, arithmetic and copies ran while one was open for 0% -> 0% of each run, Pallas kernels for 18% -> 21%
where the time goes in v3:
time: 32 us; the launch traced here: 31.8 us
  starting transfers between devices  19.4 us (61%)
  Pallas kernels  10.6 us (33%)
  waiting for transfers between devices  1.04 us (3%)
  between operations  0.72 us (2%)
    ppermute x5, starting transfers between devices, fetch(): return lax.ppermute(x, 'ctx', forth[k])  11 us
    pallas_call x7, Pallas kernels, run(): pl.pallas_call(kernel, out_shape=outs, in_specs=in_specs, out_specs=[VMEM...  10.6 us
    ppermute x5, starting transfers between devices, give_back(): return lax.ppermute(x, 'ctx', here[k])  8.45 us
    ppermute x5, waiting for transfers between devices, fetch(): return lax.ppermute(x, 'ctx', forth[k])  0.85 us
  transfers between devices with their start and end apart: 10, of which 2 were waited for; matrix products, arithmetic and copies ran while one was open for 0% of the time, Pallas kernels for 21%

profile of v3, /device:TPU:0, one launch (start us, length us, event | category | flops | bytes accessed | tf_op | source)
XLA Modules:
  0.0 31.8 jit_solution(4862472671581303457)
XLA Ops:
  0.6 0.8 %shard_map.76.pair_ref.refs_4_ = bf16[256,128]{1,0:T(8,128)(2,1)S(1)} custom-call(bf16[128,128]{1,0:T(8,128)(2,1)} %k_far.1, bf16[128,128]{1,0:T(8,128)(2,1)} %v_far.1), custom_call_target="tpu_custom_call" | custom-call | bytes 1048576 | tf_op jit(solution)/shard_map/pallas_call | solution.py:28
  1.4 4.1 %collective-permute-start.1 = (bf16[256,128]{1,0:T(8,128)(2,1)S(1)}, bf16[256,128]{1,0:T(8,128)(2,1)S(1)}, u32[]{:S(2)}, u32[]{:S(2)}) collective-permute-start(bf16[256,128]{1,0:T(8,128)(2,1)S(1)} %shard_map.76.pair_ref.refs_4_), channel_id=1, source_target_pairs={{0,16},{4,20},{8,24},{12,28},{16,0},{20,4},{24,8},{28,12},{1,17},{... | collective-permute-start | bytes 196616 | tf_op jit(solution)/shard_map/ppermute | solution.py:302
  5.5 1.3 %collective-permute-start = (bf16[256,128]{1,0:T(8,128)(2,1)S(1)}, bf16[256,128]{1,0:T(8,128)(2,1)S(1)}, u32[]{:S(2)}, u32[]{:S(2)}) collective-permute-start(bf16[256,128]{1,0:T(8,128)(2,1)S(1)} %shard_map.76.pair_ref.refs_4_), channel_id=1, source_target_pairs={{0,20},{4,24},{8,28},{12,0},{16,4},{20,8},{24,12},{28,16},{1,21},{... | collective-permute-start | bytes 196616 | tf_op jit(solution)/shard_map/ppermute | solution.py:302
  6.8 1.6 %collective-permute-start.3 = (bf16[256,128]{1,0:T(8,128)(2,1)S(1)}, bf16[256,128]{1,0:T(8,128)(2,1)S(1)}, u32[]{:S(2)}, u32[]{:S(2)}) collective-permute-start(bf16[256,128]{1,0:T(8,128)(2,1)S(1)} %shard_map.76.pair_ref.refs_4_), channel_id=1, source_target_pairs={{0,8},{4,12},{8,16},{12,20},{16,24},{20,28},{24,0},{28,4},{1,9},{5... | collective-permute-start | bytes 196616 | tf_op jit(solution)/shard_map/ppermute | solution.py:302
  8.4 1.7 %collective-permute-start.2 = (bf16[256,128]{1,0:T(8,128)(2,1)S(1)}, bf16[256,128]{1,0:T(8,128)(2,1)S(1)}, u32[]{:S(2)}, u32[]{:S(2)}) collective-permute-start(bf16[256,128]{1,0:T(8,128)(2,1)S(1)} %shard_map.76.pair_ref.refs_4_), channel_id=1, source_target_pairs={{0,12},{4,16},{8,20},{12,24},{16,28},{20,0},{24,4},{28,8},{1,13},{... | collective-permute-start | bytes 196616 | tf_op jit(solution)/shard_map/ppermute | solution.py:302
  10.0 2.4 %collective-permute-start.4 = (bf16[256,128]{1,0:T(8,128)(2,1)S(1)}, bf16[256,128]{1,0:T(8,128)(2,1)S(1)}, u32[]{:S(2)}, u32[]{:S(2)}) collective-permute-start(bf16[256,128]{1,0:T(8,128)(2,1)S(1)} %shard_map.76.pair_ref.refs_4_), channel_id=1, source_target_pairs={{0,4},{4,8},{8,12},{12,16},{16,20},{20,24},{24,28},{28,0},{1,5},{5... | collective-permute-start | bytes 196616 | tf_op jit(solution)/shard_map/ppermute | solution.py:302
  12.4 3.0 %shard_map.77 = (bf16[2048,128]{1,0:T(8,128)(2,1)S(1)}, bf16[2048,128]{1,0:T(8,128)(2,1)S(1)}, f32[128,2048]{1,0:T(8,128)S(1)}, f32[128,2048]{1,0:T(8,128)S(1)},...) custom-call(s32[1]{0:T(128)} %bitcast.start, s32[16]{0:T(128)} %lengths_far.1, bf16[2048,128]{1,0:T(8,128)(2,1)} %bitcast.4, ...), custom_call_target="tpu_custom_call" | custom-call | flops 268435456 | bytes 1048576 | tf_op jit(solution)/shard_map/pallas_call | solution.py:28
  15.4 0.0 collective-permute-done.1.refs_1_.refs_6_
  15.4 0.0 collective-permute-done.refs_0_.refs_5_
  15.4 1.1 %shard_map.78 = (f32[256,2048]{1,0:T(8,128)S(1)}, f32[256,2048]{1,0:T(8,128)S(1)}, f32[8,2048]{1,0:T(8,128)S(1)}) custom-call(bf16[2048,128]{1,0:T(8,128)(2,1)S(1)} %get-tuple-element.26.q_ref.refs_0_, bf16[2048,128]{1,0:T(8,128)(2,1)S(1)} %get-tuple-element.27.g_ref.refs_1_, f32[8,2048]{1,0:T(8,128)S(1)} %get-tuple-element.28.bound_ref.refs_2_, ...), custom_call_target="tpu_custom_call" | custom-call | flops 268435456 | bytes 1048576 | tf_op jit(solution)/shard_map/pallas_call | solution.py:28
  16.5 0.0 collective-permute-done.3.refs_1_.refs_8_
  16.5 0.8 %collective-permute-done.2.refs_0_.refs_7_ = bf16[256,128]{1,0:T(8,128)(2,1)S(1)} collective-permute-done((bf16[256,128]{1,0:T(8,128)(2,1)S(1)}, bf16[256,128]{1,0:T(8,128)(2,1)S(1)}, u32[]{:S(2)}, u32[]{:S(2)}) %collective-permute-start.2) | collective-permute-done | bytes 65568 | tf_op jit(solution)/shard_map/ppermute | solution.py:302
  17.3 1.1 %shard_map.79 = (f32[256,2048]{1,0:T(8,128)S(1)}, f32[256,2048]{1,0:T(8,128)S(1)}, f32[8,2048]{1,0:T(8,128)S(1)}) custom-call(bf16[2048,128]{1,0:T(8,128)(2,1)S(1)} %get-tuple-element.26.q_ref.refs_0_, bf16[2048,128]{1,0:T(8,128)(2,1)S(1)} %get-tuple-element.27.g_ref.refs_1_, f32[8,2048]{1,0:T(8,128)S(1)} %get-tuple-element.28.bound_ref.refs_2_, ...), custom_call_target="tpu_custom_call" | custom-call | flops 268435456 | bytes 1048576 | tf_op jit(solution)/shard_map/pallas_call | solution.py:28
  18.4 0.0 collective-permute-done.4.refs_10_.refs_9_
  18.4 2.4 %shard_map.80 = (bf16[128,2048]{1,0:T(8,128)(2,1)S(1)}, bf16[768,2048]{1,0:T(8,128)(2,1)S(1)}, bf16[256,128]{1,0:T(8,128)(2,1)S(1)}, bf16[256,128]{1,0:T(8,128)(...) custom-call(bf16[2048,128]{1,0:T(8,128)(2,1)S(1)} %get-tuple-element.26.q_ref.ref, ...), custom_call_target="tpu_custom_call" | custom-call | flops 2147483648 | bytes 1048576 | tf_op jit(solution)/shard_map/pallas_call | solution.py:28
  20.8 0.4 %collective-permute-start.5 = (bf16[256,128]{1,0:T(8,128)(2,1)S(1)}, bf16[256,128]{1,0:T(8,128)(2,1)S(1)}, u32[]{:S(2)}, u32[]{:S(2)}) collective-permute-start(bf16[256,128]{1,0:T(8,128)(2,1)S(1)} %get-tuple-element.42), channel_id=1, source_target_pairs={{20,0},{24,4},{28,8},{0,12},{4,16},{8,20},{12,24},{16,28},{21,1},{... | collective-permute-start | bytes 196616 | tf_op jit(solution)/shard_map/ppermute | solution.py:305
  21.2 1.7 %collective-permute-start.6 = (bf16[256,128]{1,0:T(8,128)(2,1)S(1)}, bf16[256,128]{1,0:T(8,128)(2,1)S(1)}, u32[]{:S(2)}, u32[]{:S(2)}) collective-permute-start(bf16[256,128]{1,0:T(8,128)(2,1)S(1)} %get-tuple-element.43), channel_id=1, source_target_pairs={{16,0},{20,4},{24,8},{28,12},{0,16},{4,20},{8,24},{12,28},{17,1},{... | collective-permute-start | bytes 196616 | tf_op jit(solution)/shard_map/ppermute | solution.py:305
  22.9 2.9 %collective-permute-start.7 = (bf16[256,128]{1,0:T(8,128)(2,1)S(1)}, bf16[256,128]{1,0:T(8,128)(2,1)S(1)}, u32[]{:S(2)}, u32[]{:S(2)}) collective-permute-start(bf16[256,128]{1,0:T(8,128)(2,1)S(1)} %get-tuple-element.44), channel_id=1, source_target_pairs={{12,0},{16,4},{20,8},{24,12},{28,16},{0,20},{4,24},{8,28},{13,1},{... | collective-permute-start | bytes 196616 | tf_op jit(solution)/shard_map/ppermute | solution.py:305
  25.9 0.9 %collective-permute-start.8 = (bf16[256,128]{1,0:T(8,128)(2,1)S(1)}, bf16[256,128]{1,0:T(8,128)(2,1)S(1)}, u32[]{:S(2)}, u32[]{:S(2)}) collective-permute-start(bf16[256,128]{1,0:T(8,128)(2,1)S(1)} %get-tuple-element.45), channel_id=1, source_target_pairs={{8,0},{12,4},{16,8},{20,12},{24,16},{28,20},{0,24},{4,28},{9,1},{1... | collective-permute-start | bytes 196616 | tf_op jit(solution)/shard_map/ppermute | solution.py:305
  26.8 2.4 %collective-permute-start.9 = (bf16[256,128]{1,0:T(8,128)(2,1)S(1)}, bf16[256,128]{1,0:T(8,128)(2,1)S(1)}, u32[]{:S(2)}, u32[]{:S(2)}) collective-permute-start(bf16[256,128]{1,0:T(8,128)(2,1)S(1)} %get-tuple-element.46), channel_id=1, source_target_pairs={{4,0},{8,4},{12,8},{16,12},{20,16},{24,20},{28,24},{0,28},{5,1},{9... | collective-permute-start | bytes 196616 | tf_op jit(solution)/shard_map/ppermute | solution.py:305
  29.2 1.7 %shard_map.81 = (bf16[2048,128]{1,0:T(8,128)(2,1)}, f32[256,128]{1,0:T(8,128)S(1)}) custom-call(bf16[2048,128]{1,0:T(8,128)(2,1)S(1)} %get-tuple-element.26.q_ref.refs_0_, bf16[2048,128]{1,0:T(8,128)(2,1)S(1)} %get-tuple-element.27.g_ref.refs_1_, bf16[128,2048]{1,0:T(8,128)(2,1)S(1)} %get-tuple-element.38.refs_2_, ...), custom_call_target="tpu_custom_call" | custom-call | flops 536870912 | bytes 1048576 | tf_op jit(solution)/shard_map/pallas_call | solution.py:28
  31.0 0.0 collective-permute-done.5.refs_0_
  31.0 0.0 collective-permute-done.6.refs_1_
  31.0 0.0 collective-permute-done.7.refs_2_
  31.0 0.0 collective-permute-done.8.refs_3_
  31.0 0.2 collective-permute-done.9.refs_4_
  31.2 0.7 %shard_map.82 = (bf16[128,128]{1,0:T(8,128)(2,1)}, bf16[128,128]{1,0:T(8,128)(2,1)}) custom-call(f32[256,128]{1,0:T(8,128)S(1)} %get-tuple-element.41.own, bf16[256,128]{1,0:T(8,128)(2,1)S(1)} %collective-permute-done.5.refs_0_, bf16[256,128]{1,0:T(8,128)(2,1)S(1)} %collective-permute-done.6.refs_1_, bf16[256,128]{1,0:T(8,128)(2,1)S(1)} %collective-permute-done.7.refs_2_, ...), custom_call_target="tpu_custom_call" | custom-call | bytes 1048576 | tf_op jit(solution)/shard_map/pallas_call | solution.py:28
Async XLA Ops:
  1.4 14.0 %collective-permute-start.1 = (bf16[256,128]{1,0:T(8,128)(2,1)S(1)}, bf16[256,128]{1,0:T(8,128)(2,1)S(1)}, u32[]{:S(2)}, u32[]{:S(2)}) collective-permute-start(bf16[256,128]{1,0:T(8,128)(2,1)S(1)} %shard_map.76.pair_ref.refs_4_), channel_id=1, source_target_pairs={{0,16},{4,20},{8,24},{12,28},{16,0},{20,4},{24,8},{28,12},{1,17},{... | collective-permute-start | bytes 196616 | tf_op jit(solution)/shard_map/ppermute | solution.py:302
  5.5 9.9 %collective-permute-start = (bf16[256,128]{1,0:T(8,128)(2,1)S(1)}, bf16[256,128]{1,0:T(8,128)(2,1)S(1)}, u32[]{:S(2)}, u32[]{:S(2)}) collective-permute-start(bf16[256,128]{1,0:T(8,128)(2,1)S(1)} %shard_map.76.pair_ref.refs_4_), channel_id=1, source_target_pairs={{0,20},{4,24},{8,28},{12,0},{16,4},{20,8},{24,12},{28,16},{1,21},{... | collective-permute-start | bytes 196616 | tf_op jit(solution)/shard_map/ppermute | solution.py:302
  6.8 9.7 %collective-permute-start.3 = (bf16[256,128]{1,0:T(8,128)(2,1)S(1)}, bf16[256,128]{1,0:T(8,128)(2,1)S(1)}, u32[]{:S(2)}, u32[]{:S(2)}) collective-permute-start(bf16[256,128]{1,0:T(8,128)(2,1)S(1)} %shard_map.76.pair_ref.refs_4_), channel_id=1, source_target_pairs={{0,8},{4,12},{8,16},{12,20},{16,24},{20,28},{24,0},{28,4},{1,9},{5... | collective-permute-start | bytes 196616 | tf_op jit(solution)/shard_map/ppermute | solution.py:302
  8.4 9.0 %collective-permute-start.2 = (bf16[256,128]{1,0:T(8,128)(2,1)S(1)}, bf16[256,128]{1,0:T(8,128)(2,1)S(1)}, u32[]{:S(2)}, u32[]{:S(2)}) collective-permute-start(bf16[256,128]{1,0:T(8,128)(2,1)S(1)} %shard_map.76.pair_ref.refs_4_), channel_id=1, source_target_pairs={{0,12},{4,16},{8,20},{12,24},{16,28},{20,0},{24,4},{28,8},{1,13},{... | collective-permute-start | bytes 196616 | tf_op jit(solution)/shard_map/ppermute | solution.py:302
  10.0 8.4 %collective-permute-start.4 = (bf16[256,128]{1,0:T(8,128)(2,1)S(1)}, bf16[256,128]{1,0:T(8,128)(2,1)S(1)}, u32[]{:S(2)}, u32[]{:S(2)}) collective-permute-start(bf16[256,128]{1,0:T(8,128)(2,1)S(1)} %shard_map.76.pair_ref.refs_4_), channel_id=1, source_target_pairs={{0,4},{4,8},{8,12},{12,16},{16,20},{20,24},{24,28},{28,0},{1,5},{5... | collective-permute-start | bytes 196616 | tf_op jit(solution)/shard_map/ppermute | solution.py:302
  20.8 10.2 %collective-permute-start.5 = (bf16[256,128]{1,0:T(8,128)(2,1)S(1)}, bf16[256,128]{1,0:T(8,128)(2,1)S(1)}, u32[]{:S(2)}, u32[]{:S(2)}) collective-permute-start(bf16[256,128]{1,0:T(8,128)(2,1)S(1)} %get-tuple-element.42), channel_id=1, source_target_pairs={{20,0},{24,4},{28,8},{0,12},{4,16},{8,20},{12,24},{16,28},{21,1},{... | collective-permute-start | bytes 196616 | tf_op jit(solution)/shard_map/ppermute | solution.py:305
  21.2 9.7 %collective-permute-start.6 = (bf16[256,128]{1,0:T(8,128)(2,1)S(1)}, bf16[256,128]{1,0:T(8,128)(2,1)S(1)}, u32[]{:S(2)}, u32[]{:S(2)}) collective-permute-start(bf16[256,128]{1,0:T(8,128)(2,1)S(1)} %get-tuple-element.43), channel_id=1, source_target_pairs={{16,0},{20,4},{24,8},{28,12},{0,16},{4,20},{8,24},{12,28},{17,1},{... | collective-permute-start | bytes 196616 | tf_op jit(solution)/shard_map/ppermute | solution.py:305
  22.9 8.0 %collective-permute-start.7 = (bf16[256,128]{1,0:T(8,128)(2,1)S(1)}, bf16[256,128]{1,0:T(8,128)(2,1)S(1)}, u32[]{:S(2)}, u32[]{:S(2)}) collective-permute-start(bf16[256,128]{1,0:T(8,128)(2,1)S(1)} %get-tuple-element.44), channel_id=1, source_target_pairs={{12,0},{16,4},{20,8},{24,12},{28,16},{0,20},{4,24},{8,28},{13,1},{... | collective-permute-start | bytes 196616 | tf_op jit(solution)/shard_map/ppermute | solution.py:305
  25.9 5.1 %collective-permute-start.8 = (bf16[256,128]{1,0:T(8,128)(2,1)S(1)}, bf16[256,128]{1,0:T(8,128)(2,1)S(1)}, u32[]{:S(2)}, u32[]{:S(2)}) collective-permute-start(bf16[256,128]{1,0:T(8,128)(2,1)S(1)} %get-tuple-element.45), channel_id=1, source_target_pairs={{8,0},{12,4},{16,8},{20,12},{24,16},{28,20},{0,24},{4,28},{9,1},{1... | collective-permute-start | bytes 196616 | tf_op jit(solution)/shard_map/ppermute | solution.py:305
  26.8 4.3 %collective-permute-start.9 = (bf16[256,128]{1,0:T(8,128)(2,1)S(1)}, bf16[256,128]{1,0:T(8,128)(2,1)S(1)}, u32[]{:S(2)}, u32[]{:S(2)}) collective-permute-start(bf16[256,128]{1,0:T(8,128)(2,1)S(1)} %get-tuple-element.46), channel_id=1, source_target_pairs={{4,0},{8,4},{12,8},{16,12},{20,16},{24,20},{28,24},{0,28},{5,1},{9... | collective-permute-start | bytes 196616 | tf_op jit(solution)/shard_map/ppermute | solution.py:305
